TPU v7x, 32 devices: a whole 2x2x4 slice. The times are simulated.
32 devices in a mesh: gx: 8 (over z, y), gy: 4 (over x, core).
Axes of the slice: x: 2, y: 2, z: 4, core: 2. Of those that a mesh axis runs over, the one named last changes fastest.
Arguments:
- base_state: bfloat16 [2, 256, 1024], P(None, 'gy', 'gx'), may hold values from -6 to 6
- increment: bfloat16 [2, 256, 1024], P(None, 'gy', 'gx'), may hold values from -6 to 6
- cotangent: bfloat16 [256, 1024], P('gy', 'gx'), may hold values from -24 to 24
- land_sea: int32 [256, 1024], P('gy', 'gx'), may hold values 0 or 1
- storage: float32 [256, 1024], P('gy', 'gx'), may hold values from 0.25 to 4
- source: float32 [256, 1024], P('gy', 'gx'), may hold values from -100 to 100
- w_first: bfloat16 [25, 128], replicated, may hold values from -0.875 to 0.875
- w_middle_one: bfloat16 [25, 4096], replicated, may hold values from -0.15625 to 0.15625
- w_middle_two: bfloat16 [25, 4096], replicated, may hold values from -0.15625 to 0.15625
- w_last: bfloat16 [25, 64], replicated, may hold values from -0.15625 to 0.15625
Outputs:
- adjoint_gradient: float32 [2, 256, 1024], P(None, 'gy', 'gx')
- surface: float32 [256, 1024], P('gy', 'gx')
- residual: float32 [256, 1024], P('gy', 'gx')
All inputs are finite; a program needn't handle non-finite values. No bound on the sum of `land_sea` on one device may be relied on, other than what follows from the above.
Results may differ from a plain program's by a relative error of at most 0.0051.
Values may be sent and summed in bfloat16 or wider, within the bound.
No kernel may reach another device: no remote copies, remote signals or barrier semaphores. Data moves between devices by JAX's collectives and lax.ppermute only.
A program may use at most 128 MiB of HBM per device.

v0:
```python
import jax
import jax.numpy as jnp
from jax import lax
from jax.sharding import PartitionSpec as P

ITERS = 3


def with_halo(cells, sides, width):
    for axis, dim in sides:
        count = lax.axis_size(axis)
        head = lax.slice_in_dim(cells, 0, width, axis=dim)
        tail = lax.slice_in_dim(cells, cells.shape[dim] - width, cells.shape[dim], axis=dim)
        cells = jnp.concatenate(
            [
                lax.ppermute(tail, axis, [(i, (i + 1) % count) for i in range(count)]),
                cells,
                lax.ppermute(head, axis, [((i + 1) % count, i) for i in range(count)]),
            ],
            axis=dim,
        )
    return cells


def close_rows(padded, width):
    count = lax.axis_size("gy")
    place = lax.axis_index("gy")
    total_rows = padded.shape[-2]
    position = jnp.arange(total_rows)
    outside = (position < width) & (place == 0) | (position >= total_rows - width) & (
        place == count - 1
    )
    return jnp.where(outside[:, None], jnp.zeros((), padded.dtype), padded)


def shaped(table, inputs):
    return table.reshape(5, 5, inputs, table.shape[1] // inputs)


def convolve(padded, kernel):
    return lax.conv_general_dilated(
        padded,
        kernel,
        (1, 1),
        "VALID",
        dimension_numbers=("NCHW", "HWIO", "NCHW"),
        preferred_element_type=jnp.float32,
    )


def turned(kernel):
    return jnp.flip(kernel, (0, 1)).transpose(0, 1, 3, 2)


def layer_edges(field):
    return close_rows(with_halo(field, (("gx", 3), ("gy", 2)), 2), 2)


def adjoint_edges(field):
    return close_rows(with_halo(field, (("gx", 3), ("gy", 2)), 2), 2)


def faces_of(border):
    own = border[1:-1, 1:-1]
    return (
        own * border[1:-1, 2:],
        own * border[1:-1, :-2],
        own * border[2:, 1:-1],
        own * border[:-2, 1:-1],
    )


def laplace(field, storage, faces):
    rim = close_rows(with_halo(field, (("gx", 1), ("gy", 0)), 1), 1)
    east, west, north, south = faces
    total = storage * field + east * (field - rim[1:-1, 2:]) + west * (field - rim[1:-1, :-2])
    return total + north * (field - rim[2:, 1:-1]) + south * (field - rim[:-2, 1:-1])


def squares(residual):
    return lax.psum(jnp.sum(residual * residual), ("gx", "gy"))


def shards(
    base_state,
    increment,
    cotangent,
    land_sea,
    storage,
    source,
    w_first,
    w_middle_one,
    w_middle_two,
    w_last,
):
    hidden = w_last.shape[1]
    k_first = shaped(w_first, 2)
    k_one = shaped(w_middle_one, hidden)
    k_two = shaped(w_middle_two, hidden)
    k_last = shaped(w_last, hidden)
    mask = land_sea.astype(jnp.float32)
    stacked = jnp.concatenate([base_state, increment, land_sea.astype(jnp.bfloat16)[None]], 0)[None]
    padded = layer_edges(stacked)
    border = padded[0, 4, 1:-1, 1:-1].astype(jnp.float32)
    pre_act = convolve(jnp.stack([padded[0, 0:2], padded[0, 2:4]]), k_first)
    slope_one = jnp.tanh(pre_act[0])
    act_one = (mask * slope_one).astype(jnp.bfloat16)
    tl_one = (mask * (1.0 - slope_one * slope_one) * pre_act[1]).astype(jnp.bfloat16)
    pre_act = convolve(layer_edges(jnp.stack([act_one, tl_one])), k_one)
    slope_two = jnp.tanh(pre_act[0])
    act_two = (mask * slope_two).astype(jnp.bfloat16)
    tl_two = (mask * (1.0 - slope_two * slope_two) * pre_act[1]).astype(jnp.bfloat16)
    pre_act = convolve(layer_edges(jnp.stack([act_two, tl_two])), k_two)
    slope_three = jnp.tanh(pre_act[0])
    tl_three = (mask * (1.0 - slope_three * slope_three) * pre_act[1]).astype(jnp.bfloat16)
    last_out = convolve(layer_edges(tl_three[None]), k_last)[0, 0]
    tl_force = mask * last_out
    masked_cot = (mask * cotangent.astype(jnp.float32)).astype(jnp.bfloat16)
    back_act = convolve(adjoint_edges(masked_cot[None, None]), turned(k_last))[0]
    back_three = (mask * (1.0 - slope_three * slope_three) * back_act).astype(jnp.bfloat16)
    back_act = convolve(adjoint_edges(back_three[None]), turned(k_two))[0]
    back_two = (mask * (1.0 - slope_two * slope_two) * back_act).astype(jnp.bfloat16)
    back_act = convolve(adjoint_edges(back_two[None]), turned(k_one))[0]
    back_one = (mask * (1.0 - slope_one * slope_one) * back_act).astype(jnp.bfloat16)
    adjoint_gradient = convolve(adjoint_edges(back_one[None]), turned(k_first))[0]
    faces = faces_of(border)
    rhs = source + tl_force
    surface = jnp.zeros_like(rhs)
    residual = rhs
    direction = rhs
    norm_now = squares(residual)
    for step in range(ITERS):
        image = laplace(direction, storage, faces)
        alpha = norm_now / lax.psum(jnp.sum(direction * image), ("gx", "gy"))
        surface = surface + alpha * direction
        residual = residual - alpha * image
        norm_next = squares(residual)
        direction = residual + norm_next / norm_now * direction
        norm_now = norm_next
    return (adjoint_gradient, surface, residual)


def solution(mesh):
    placed = (
        P(None, "gy", "gx"),
        P(None, "gy", "gx"),
        P("gy", "gx"),
        P("gy", "gx"),
        P("gy", "gx"),
        P("gy", "gx"),
        P(),
        P(),
        P(),
        P(),
    )
    return jax.shard_map(
        shards,
        mesh=mesh,
        in_specs=placed,
        out_specs=(P(None, "gy", "gx"), P("gy", "gx"), P("gy", "gx")),
        check_vma=False,
    )
```

profile of v0, /device:TPU:0, one launch (start us, length us, event | category | flops | bytes accessed | tf_op | source)
XLA Modules:
  0.0 691.9 jit_solution(9050099003287172005)
XLA Ops:
  3.4 3.0 collective-permute-start
  6.4 3.1 collective-permute-start.1
  10.4 4.7 collective-permute-start.13
  21.6 3.1 collective-permute-done.2
  27.2 7.8 %broadcast_select_fusion.2 = f32[64,16,17,64]{3,1,2,0:T(8,128)} fusion(pred[16,17]{0,1:T(8,128)(4,1)S(1)} %copy-done.18, bf16[2,68,16,21]{2,0,3,1:T(2,128)(2,1)S(1)} %copy.22, bf16[5,5,2,64]{3,2,1,0:T(2,128)(2,1)S(1)} %reshape.286), kind=kOutput, calls=%fused_computation.23 | convolution fusion | flops 112525312 | bytes 4554512 | tf_op jit(solution)/shard_map/conv_general_dilated | solution.py:41
  35.0 6.4 copy.23
  46.5 4.7 collective-permute-start.5
  60.2 8.8 %fusion.12 = bf16[64,68,2,132]{0,1,3,2:T(8,128)(2,1)} fusion(bf16[2,64,2,132]{1,2,3,0:T(2,128)(2,1)} %collective-permute-done.7, bf16[2,64,64,2]{1,2,3,0:T(8,128)(2,1)S(1)} %collective-permute-done.5, bf16[1,64,64,128]{1,2,3,0:T(8,128)(2,1)} %copy-done.2, bf16[1,64,64,128]{1,2,3,0:T(8,128)(2,1)S(1)} %get-tuple-element.21, ...), kind=kLoop, calls=%fused_computation.18 | loop fusion | flops 14936064 | bytes 4595780 | tf_op jit(solution)/shard_map/jit(_where)/select_n | solution.py:33
  69.0 6.8 copy.70
  75.8 3.4 pad.2.clone
  79.3 4.5 fusion.10
  83.8 9.8 %copy.25 = bf16[64,68,2,8,21]{0,3,2,4,1:T(8,128)(2,1)} copy(bf16[64,68,2,8,21]{1,0,4,3,2:T(8,128)(2,1)} %fusion.10) | data formatting | bytes 5849088 | tf_op jit(solution)/shard_map/conv_general_dilated | solution.py:41
  93.6 18.0 %broadcast_select_fusion.1 = f32[64,16,17,64]{3,1,2,0:T(8,128)S(1)} fusion(pred[16,17]{0,1:T(8,128)(4,1)S(1)} %copy-done.18, bf16[5,5,64,64]{3,2,1,0:T(8,128)(2,1)S(1)} %reshape.287, bf16[64,68,2,8,21]{0,3,2,4,1:T(8,128)(2,1)} %copy.25), kind=kOutput, calls=%fused_computation.22 | convolution fusion | flops 3566272512 | bytes 7586064 | tf_op jit(solution)/shard_map/conv_general_dilated | solution.py:41
  111.6 2.9 copy.26
  116.2 11.2 %multiply_convert_fusion = (bf16[1,64,64,128]{1,2,3,0:T(8,128)(2,1)S(1)}, bf16[1,64,64,128]{1,2,3,0:T(8,128)(2,1)S(1)}) fusion(f32[2,64,64,128]{1,2,3,0:T(8,128)S(1)} %slice_bitcast_fusion.1, f32[64,128]{0,1:T(8,128)S(1)} %get-tuple-element.65), kind=kLoop, calls=%fused_computation.45 | loop fusion | flops 3670016 | bytes 6324224 | tf_op jit(solution)/shard_map/convert_element_type | solution.py:111
  129.4 4.7 collective-permute-start.9
  140.1 6.5 broadcast_select_fusion.6
  146.6 2.8 copy.34
  149.4 7.7 %fusion.13 = bf16[64,68,2,132]{0,1,3,2:T(8,128)(2,1)} fusion(bf16[2,64,2,132]{1,2,3,0:T(2,128)(2,1)S(1)} %collective-permute-done.11, bf16[2,64,64,2]{1,2,3,0:T(8,128)(2,1)S(1)} %collective-permute-done.9, bf16[1,64,64,128]{1,2,3,0:T(8,128)(2,1)S(1)} %copy-done.4, bf16[1,64,64,128]{1,2,3,0:T(8,128)(2,1)S(1)} %get-tuple-element.19, ...), kind=kLoop, calls=%fused_computation.20 | loop fusion | flops 14936064 | bytes 4595780 | tf_op jit(solution)/shard_map/jit(_where)/select_n | solution.py:33
  157.1 6.8 copy.71
  163.9 3.4 pad.4.clone
  167.3 4.5 fusion.11
  171.8 9.9 %copy.28 = bf16[64,68,2,8,21]{0,3,2,4,1:T(8,128)(2,1)} copy(bf16[64,68,2,8,21]{1,0,4,3,2:T(8,128)(2,1)} %fusion.11) | data formatting | bytes 5849088 | tf_op jit(solution)/shard_map/conv_general_dilated | solution.py:41
  181.7 18.4 %broadcast_select_fusion = f32[64,16,17,64]{3,1,2,0:T(8,128)S(1)} fusion(pred[16,17]{0,1:T(8,128)(4,1)S(1)} %copy-done.18, bf16[5,5,64,64]{3,2,1,0:T(8,128)(2,1)S(1)} %reshape.288, bf16[64,68,2,8,21]{0,3,2,4,1:T(8,128)(2,1)} %copy.28), kind=kOutput, calls=%fused_computation.21 | convolution fusion | flops 3566272512 | bytes 7586064 | tf_op jit(solution)/shard_map/conv_general_dilated | solution.py:41
  200.1 2.9 copy.29
  204.6 4.0 fusion.14
  208.7 5.0 collective-permute-start.17
  217.5 4.8 collective-permute-start.29
  222.3 4.1 fusion.55
  227.4 17.8 %broadcast_select_fusion.5 = f32[64,8,17,64]{3,1,2,0:T(8,128)S(1)} fusion(pred[8,17]{0,1:T(8,128)(4,1)S(1)} %copy-done.17, bf16[5,5,64,64]{3,2,1,0:T(8,128)(2,1)S(1)} %reshape.288, bf16[64,68,1,7,4]{0,3,4,1,2:T(8,128)(2,1)S(1)} %slice.321, bf16[64,68,1,8,17]{0,3,4,1,2:T(8,128)(2,1)S(1)} %copy.37), kind=kOutput, calls=%fused_computation.80 | convolution fusion | flops 1787523072 | bytes 3860616 | tf_op jit(solution)/shard_map/conv_general_dilated | solution.py:41
  247.9 4.7 collective-permute-start.21
  259.0 8.2 %fusion.58 = (bf16[64,68,1,132]{0,1,3,2:T(8,128)(2,1)S(1)}, bf16[64,68,1,132]{0,1,3,2:T(8,128)(2,1)}) fusion(bf16[1,64,2,132]{1,2,3,0:T(2,128)(2,1)S(1)} %collective-permute-done.31, bf16[1,64,64,2]{1,2,3,0:T(8,128)(2,1)S(1)} %collective-permute-done.29, bf16[1,64,64,128]{1,2,3,0:T(8,128)(2,1)} %copy-done.5, ...), kind=kLoop, calls=%fused_computation.77 | loop fusion | flops 12638208 | bytes 4595780 | tf_op jit(solution)/shard_map/jit(_where)/select_n | solution.py:33
  268.5 17.1 %broadcast_select_fusion.3 = f32[64,8,17,1]{3,1,2,0:T(8,128)} fusion(pred[8,17]{0,1:T(8,128)(4,1)S(1)} %copy-done.17, bf16[64,68,1,7,4]{0,3,4,1,2:T(8,128)(2,1)S(1)} %slice.334, bf16[64,68,1,8,17]{0,3,4,1,2:T(8,128)(2,1)S(1)} %copy.49, bf16[5,5,64,1]{2,1,0,3:T(8,128)(2,1)S(1)} %copy-done.12), kind=kOutput, calls=%fused_computation.78 | convolution fusion | flops 32248320 | bytes 1465608 | tf_op jit(solution)/shard_map/conv_general_dilated | solution.py:41
  285.5 3.3 copy.51
  289.0 4.7 collective-permute-start.33
  300.0 39.9 %all-reduce = (f32[]{:T(128)}, f32[]{:T(128)}) all-reduce(f32[]{:T(128)} %get-tuple-element.7, f32[]{:T(128)} %get-tuple-element.6), channel_id=1, replica_groups=mesh['gx'=8,'gy'=4] {'gx','gy'}, use_global_device_ids=true, to_apply=%region_1.2 | all-reduce | flops 2 | bytes 16 | tf_op jit(solution)/shard_map/psum | solution.py:81
  341.8 41.6 %psum.44 = f32[]{:T(128)} all-reduce(f32[]{:T(128)} %multiply_reduce_fusion.3), channel_id=1, replica_groups=mesh['gx'=8,'gy'=4] {'gx','gy'}, use_global_device_ids=true, to_apply=%region_5.6 | all-reduce | flops 1 | bytes 8 | tf_op jit(solution)/shard_map/psum | solution.py:81
  384.8 2.5 collective-permute-start.36
  394.3 15.9 %broadcast_select_fusion.4 = f32[64,8,17,64]{3,1,2,0:T(8,128)S(1)} fusion(pred[8,17]{0,1:T(8,128)(4,1)S(1)} %copy-done.17, bf16[5,5,64,64]{3,2,1,0:T(8,128)(2,1)S(1)} %copy-done.10, bf16[64,68,1,7,4]{0,3,4,1,2:T(8,128)(2,1)S(1)} %slice.325, bf16[64,68,1,8,17]{0,3,4,1,2:T(8,128)(2,1)S(1)} %copy.41), kind=kOutput, calls=%fused_computation.79 | convolution fusion | flops 1787523072 | bytes 3860616 | tf_op jit(solution)/shard_map/conv_general_dilated | solution.py:41
  410.2 3.0 copy.42
  414.1 39.9 %psum.45 = f32[]{:T(128)} all-reduce(f32[]{:T(128)} %get-tuple-element.14), channel_id=1, replica_groups=mesh['gx'=8,'gy'=4] {'gx','gy'}, use_global_device_ids=true, to_apply=%region_7.8 | all-reduce | flops 1 | bytes 8 | tf_op jit(solution)/shard_map/psum | solution.py:134
  456.0 40.7 %psum.46 = f32[]{:T(128)} all-reduce(f32[]{:T(128)} %get-tuple-element.12), channel_id=1, replica_groups=mesh['gx'=8,'gy'=4] {'gx','gy'}, use_global_device_ids=true, to_apply=%region_9.10 | all-reduce | flops 1 | bytes 8 | tf_op jit(solution)/shard_map/psum | solution.py:81
  498.1 2.5 collective-permute-start.40
  502.8 4.2 fusion.16
  509.0 4.7 collective-permute-start.25
  514.6 37.4 %psum.47 = f32[]{:T(128)} all-reduce(f32[]{:T(128)} %get-tuple-element.10), channel_id=1, replica_groups=mesh['gx'=8,'gy'=4] {'gx','gy'}, use_global_device_ids=true, to_apply=%region_11.12 | all-reduce | flops 1 | bytes 8 | tf_op jit(solution)/shard_map/psum | solution.py:134
  557.8 3.9 fusion.57
  562.9 127.1 %fusion.69 = f32[64,8,17,2]{1,3,2,0:T(2,128)S(1)} fusion(bf16[5,5,2,64]{3,2,1,0:T(2,128)(2,1)S(1)} %copy-done.16, bf16[64,68,1,7,4]{0,3,4,1,2:T(8,128)(2,1)S(1)} %slice.329, bf16[64,68,1,8,17]{0,3,4,1,2:T(8,128)(2,1)S(1)} %copy.45, pred[8,17]{0,1:T(8,128)(4,1)S(1)} %copy-done.17), kind=kOutput, calls=%fused_computation.86 | convolution fusion | flops 60109824 | bytes 1503624 | tf_op jit(solution)/shard_map/conv_general_dilated | solution.py:41
  (215 shorter events, 80.7 us)
Async XLA Ops:
  0.6 26.6 %copy-start.18 = (pred[16,17]{0,1:T(8,128)(4,1)S(1)}, pred[16,17]{0,1:T(8,128)(4,1)}, u32[]{:S(2)}) copy-start(pred[16,17]{0,1:T(8,128)(4,1)} %constant.55) | copy-start | bytes 820
  1.5 33.5 %copy-start.6 = (s32[64,128]{0,1:T(8,128)}, s32[64,128]{0,1:T(8,128)S(1)}, u32[]{:S(2)}) copy-start(s32[64,128]{0,1:T(8,128)S(1)} %copy.16) | copy-start | bytes 98308
  3.4 16.2 %collective-permute-start = (bf16[1,5,64,2]{2,3,1,0:T(2,128)(2,1)S(1)}, bf16[1,5,64,2]{2,3,1,0:T(2,128)(2,1)S(1)}, u32[]{:S(2)}, u32[]{:S(2)}) collective-permute-start(bf16[1,5,64,2]{2,3,1,0:T(2,128)(2,1)S(1)} %get-tuple-element.51), channel_id=1, source_target_pairs={{0,4},{4,8},{8,12},{12,16},{16,20},{20,24},{24,28},{28,0},{1,5},{5... | collective-permute-start | bytes 3848 | tf_op jit(solution)/shard_map/ppermute | solution.py:16
  6.4 13.2 %collective-permute-start.1 = (bf16[1,5,64,2]{2,3,1,0:T(2,128)(2,1)S(1)}, bf16[1,5,64,2]{2,3,1,0:T(2,128)(2,1)S(1)}, u32[]{:S(2)}, u32[]{:S(2)}) collective-permute-start(bf16[1,5,64,2]{2,3,1,0:T(2,128)(2,1)S(1)} %get-tuple-element.52), channel_id=1, source_target_pairs={{4,0},{8,4},{12,8},{16,12},{20,16},{24,20},{28,24},{0,28},{5,1},{9... | collective-permute-start | bytes 3848 | tf_op jit(solution)/shard_map/ppermute | solution.py:18
  10.4 11.2 %collective-permute-start.12 = (bf16[1,1,64,2]{2,3,1,0:T(2,128)(2,1)S(1)}, bf16[1,1,64,2]{2,3,1,0:T(2,128)(2,1)S(1)}, u32[]{:S(2)}, u32[]{:S(2)}) collective-permute-start(bf16[1,1,64,2]{2,3,1,0:T(2,128)(2,1)S(1)} %get-tuple-element.69), channel_id=1, source_target_pairs={{0,4},{4,8},{8,12},{12,16},{16,20},{20,24},{24,28},{28,0},{1,5},{5... | collective-permute-start | bytes 776 | tf_op jit(solution)/shard_map/ppermute | solution.py:16
  10.4 11.2 %collective-permute-start.13 = (bf16[1,1,64,2]{2,3,1,0:T(2,128)(2,1)S(1)}, bf16[1,1,64,2]{2,3,1,0:T(2,128)(2,1)S(1)}, u32[]{:S(2)}, u32[]{:S(2)}) collective-permute-start(bf16[1,1,64,2]{2,3,1,0:T(2,128)(2,1)S(1)} %get-tuple-element.70), channel_id=1, source_target_pairs={{4,0},{8,4},{12,8},{16,12},{20,16},{24,20},{28,24},{0,28},{5,1},{9... | collective-permute-start | bytes 776 | tf_op jit(solution)/shard_map/ppermute | solution.py:18
  17.3 76.3 %copy-start.9 = (bf16[5,5,64,64]{3,2,1,0:T(8,128)(2,1)}, bf16[5,5,64,64]{3,2,1,0:T(8,128)(2,1)S(1)}, u32[]{:S(2)}) copy-start(bf16[5,5,64,64]{3,2,1,0:T(8,128)(2,1)S(1)} %reshape.287) | copy-start | bytes 614404
  19.8 4.9 collective-permute-start.2
  19.9 5.8 collective-permute-start.3
  46.4 7.5 %collective-permute-start.4 = (bf16[2,64,64,2]{1,2,3,0:T(8,128)(2,1)S(1)}, bf16[2,64,64,2]{1,2,3,0:T(8,128)(2,1)S(1)}, u32[]{:S(2)}, u32[]{:S(2)}) collective-permute-start(bf16[2,64,64,2]{1,2,3,0:T(8,128)(2,1)S(1)} %get-tuple-element.29), channel_id=1, source_target_pairs={{0,4},{4,8},{8,12},{12,16},{16,20},{20,24},{24,28},{28,0},{1,5},{5... | collective-permute-start | bytes 98312 | tf_op jit(solution)/shard_map/ppermute | solution.py:16
  46.5 7.4 %collective-permute-start.5 = (bf16[2,64,64,2]{1,2,3,0:T(8,128)(2,1)S(1)}, bf16[2,64,64,2]{1,2,3,0:T(8,128)(2,1)S(1)}, u32[]{:S(2)}, u32[]{:S(2)}) collective-permute-start(bf16[2,64,64,2]{1,2,3,0:T(8,128)(2,1)S(1)} %get-tuple-element.30), channel_id=1, source_target_pairs={{4,0},{8,4},{12,8},{16,12},{20,16},{24,20},{28,24},{0,28},{5,1},{9... | collective-permute-start | bytes 98312 | tf_op jit(solution)/shard_map/ppermute | solution.py:18
  51.3 5.6 collective-permute-start.14
  51.4 5.4 collective-permute-start.15
  54.9 4.6 collective-permute-start.6
  54.9 5.3 collective-permute-start.7
  129.4 7.5 %collective-permute-start.8 = (bf16[2,64,64,2]{1,2,3,0:T(8,128)(2,1)}, bf16[2,64,64,2]{1,2,3,0:T(8,128)(2,1)S(1)}, u32[]{:S(2)}, u32[]{:S(2)}) collective-permute-start(bf16[2,64,64,2]{1,2,3,0:T(8,128)(2,1)} %get-tuple-element.27), channel_id=1, source_target_pairs={{0,4},{4,8},{8,12},{12,16},{16,20},{20,24},{24,28},{28,0},{1,5},{5... | collective-permute-start | bytes 98312 | tf_op jit(solution)/shard_map/ppermute | solution.py:16
  129.4 7.5 %collective-permute-start.9 = (bf16[2,64,64,2]{1,2,3,0:T(8,128)(2,1)}, bf16[2,64,64,2]{1,2,3,0:T(8,128)(2,1)S(1)}, u32[]{:S(2)}, u32[]{:S(2)}) collective-permute-start(bf16[2,64,64,2]{1,2,3,0:T(8,128)(2,1)} %get-tuple-element.28), channel_id=1, source_target_pairs={{4,0},{8,4},{12,8},{16,12},{20,16},{24,20},{28,24},{0,28},{5,1},{9... | collective-permute-start | bytes 98312 | tf_op jit(solution)/shard_map/ppermute | solution.py:18
  138.2 11.2 %collective-permute-start.10 = (bf16[2,64,2,132]{1,2,3,0:T(2,128)(2,1)S(1)}, bf16[2,64,2,132]{1,2,3,0:T(2,128)(2,1)S(1)}, u32[]{:S(2)}, u32[]{:S(2)}) collective-permute-start(bf16[2,64,2,132]{1,2,3,0:T(2,128)(2,1)S(1)} %get-tuple-element.23), channel_id=1, source_target_pairs={{0,1},{1,2},{2,3},{3,0},{4,5},{5,6},{6,7},{7,4},{8,9},{9,10},{10,1... | collective-permute-start | bytes 202760 | tf_op jit(solution)/shard_map/ppermute | solution.py:16
  138.5 10.9 %collective-permute-start.11 = (bf16[2,64,2,132]{1,2,3,0:T(2,128)(2,1)S(1)}, bf16[2,64,2,132]{1,2,3,0:T(2,128)(2,1)S(1)}, u32[]{:S(2)}, u32[]{:S(2)}) collective-permute-start(bf16[2,64,2,132]{1,2,3,0:T(2,128)(2,1)S(1)} %get-tuple-element.24), channel_id=1, source_target_pairs={{1,0},{2,1},{3,2},{0,3},{5,4},{6,5},{7,6},{4,7},{9,8},{10,9},{11,1... | collective-permute-start | bytes 202760 | tf_op jit(solution)/shard_map/ppermute | solution.py:18
  208.6 44.0 %copy-start.5 = (bf16[1,64,64,128]{1,2,3,0:T(8,128)(2,1)}, bf16[1,64,64,128]{1,2,3,0:T(8,128)(2,1)S(1)}, u32[]{:S(2)}) copy-start(bf16[1,64,64,128]{1,2,3,0:T(8,128)(2,1)S(1)} %get-tuple-element.17) | copy-start | bytes 3145732
  208.7 6.8 collective-permute-start.16
  208.7 6.8 collective-permute-start.17
  215.7 6.6 collective-permute-start.18
  215.7 6.6 collective-permute-start.19
  217.5 35.2 %collective-permute-start.28 = (bf16[1,64,64,2]{1,2,3,0:T(8,128)(2,1)S(1)}, bf16[1,64,64,2]{1,2,3,0:T(8,128)(2,1)S(1)}, u32[]{:S(2)}, u32[]{:S(2)}) collective-permute-start(bf16[1,64,64,2]{1,2,3,0:T(8,128)(2,1)S(1)} %get-tuple-element.39), channel_id=1, source_target_pairs={{0,4},{4,8},{8,12},{12,16},{16,20},{20,24},{24,28},{28,0},{1,5},{5... | collective-permute-start | bytes 49160 | tf_op jit(solution)/shard_map/ppermute | solution.py:16
  217.5 35.2 %collective-permute-start.29 = (bf16[1,64,64,2]{1,2,3,0:T(8,128)(2,1)S(1)}, bf16[1,64,64,2]{1,2,3,0:T(8,128)(2,1)S(1)}, u32[]{:S(2)}, u32[]{:S(2)}) collective-permute-start(bf16[1,64,64,2]{1,2,3,0:T(8,128)(2,1)S(1)} %get-tuple-element.40), channel_id=1, source_target_pairs={{4,0},{8,4},{12,8},{16,12},{20,16},{24,20},{28,24},{0,28},{5,1},{9... | collective-permute-start | bytes 49160 | tf_op jit(solution)/shard_map/ppermute | solution.py:18
  247.9 6.7 collective-permute-start.20
  247.9 6.7 collective-permute-start.21
  252.8 3.9 collective-permute-start.30
  252.9 3.8 collective-permute-start.31
  254.7 4.3 collective-permute-start.22
  254.8 4.2 collective-permute-start.23
  288.9 6.3 collective-permute-start.32
  289.0 6.2 collective-permute-start.33
  295.3 3.8 collective-permute-start.34
  295.4 3.6 collective-permute-start.35
  384.8 7.4 %collective-permute-start.36 = (f32[64,1]{0,1:T(1,128)S(1)}, f32[64,1]{0,1:T(1,128)S(1)}, u32[]{:S(2)}, u32[]{:S(2)}) collective-permute-start(f32[64,1]{0,1:T(1,128)S(1)} %get-tuple-element.61), channel_id=1, source_target_pairs={{0,4},{4,8},{8,12},{12,16},{16,20},{20,24},{24,28},{28,0},{1,5},{5... | collective-permute-start | bytes 776 | tf_op jit(solution)/shard_map/ppermute | solution.py:16
  387.4 4.9 collective-permute-start.37
  392.4 20.8 %collective-permute-start.38 = (f32[1,130]{0,1:T(8,128)S(1)}, f32[1,130]{0,1:T(8,128)S(1)}, u32[]{:S(2)}, u32[]{:S(2)}) collective-permute-start(f32[1,130]{0,1:T(8,128)S(1)} %get-tuple-element.55), channel_id=1, source_target_pairs={{0,1},{1,2},{2,3},{3,0},{4,5},{5,6},{6,7},{7,4},{8,9},{9,10},{10,1... | collective-permute-start | bytes 1568 | tf_op jit(solution)/shard_map/ppermute | solution.py:16
  392.5 20.8 %collective-permute-start.39 = (f32[1,130]{0,1:T(8,128)S(1)}, f32[1,130]{0,1:T(8,128)S(1)}, u32[]{:S(2)}, u32[]{:S(2)}) collective-permute-start(f32[1,130]{0,1:T(8,128)S(1)} %get-tuple-element.56), channel_id=1, source_target_pairs={{1,0},{2,1},{3,2},{0,3},{5,4},{6,5},{7,6},{4,7},{9,8},{10,9},{11,1... | collective-permute-start | bytes 1568 | tf_op jit(solution)/shard_map/ppermute | solution.py:18
  498.1 9.0 %collective-permute-start.40 = (f32[64,1]{0,1:T(1,128)S(1)}, f32[64,1]{0,1:T(1,128)S(1)}, u32[]{:S(2)}, u32[]{:S(2)}) collective-permute-start(f32[64,1]{0,1:T(1,128)S(1)} %get-tuple-element.59), channel_id=1, source_target_pairs={{0,4},{4,8},{8,12},{12,16},{16,20},{20,24},{24,28},{28,0},{1,5},{5... | collective-permute-start | bytes 776 | tf_op jit(solution)/shard_map/ppermute | solution.py:16
  500.6 6.5 collective-permute-start.41
  507.2 6.5 collective-permute-start.42
  507.2 6.5 collective-permute-start.43
  509.0 44.3 %collective-permute-start.24 = (bf16[1,64,64,2]{1,2,3,0:T(8,128)(2,1)S(1)}, bf16[1,64,64,2]{1,2,3,0:T(8,128)(2,1)S(1)}, u32[]{:S(2)}, u32[]{:S(2)}) collective-permute-start(bf16[1,64,64,2]{1,2,3,0:T(8,128)(2,1)S(1)} %get-tuple-element.41), channel_id=1, source_target_pairs={{0,4},{4,8},{8,12},{12,16},{16,20},{20,24},{24,28},{28,0},{1,5},{5... | collective-permute-start | bytes 49160 | tf_op jit(solution)/shard_map/ppermute | solution.py:16
  509.0 44.4 %collective-permute-start.25 = (bf16[1,64,64,2]{1,2,3,0:T(8,128)(2,1)S(1)}, bf16[1,64,64,2]{1,2,3,0:T(8,128)(2,1)S(1)}, u32[]{:S(2)}, u32[]{:S(2)}) collective-permute-start(bf16[1,64,64,2]{1,2,3,0:T(8,128)(2,1)S(1)} %get-tuple-element.42), channel_id=1, source_target_pairs={{4,0},{8,4},{12,8},{16,12},{20,16},{24,20},{28,24},{0,28},{5,1},{9... | collective-permute-start | bytes 49160 | tf_op jit(solution)/shard_map/ppermute | solution.py:18
  553.5 3.8 collective-permute-start.26
  553.5 4.2 collective-permute-start.27
  (17 other events, 126.5 us)
where the time goes:
time: 700 us; the launch traced here: 692 us
  matrix products  229 us (33%)
  blocking collectives  199 us (28%)
  local copies, waits for them, and re-layouts  89.9 us (13%)
  starting transfers between devices  74 us (11%)
  other arithmetic  73.7 us (11%)
  waiting for transfers between devices  17.7 us (3%)
  between operations  8.55 us (1%)
    conv_general_dilated x8, matrix products, convolve(): lax.conv_general_dilated(padded, kernel, (1, 1), 'VALID', dimension_numbe...  229 us
    psum x3, blocking collectives, squares(): return lax.psum(jnp.sum(residual * residual), ('gx', 'gy'))  122 us
    psum x2, blocking collectives, shards(): alpha = norm_now / lax.psum(jnp.sum(direction * image), ('gx', 'gy'))  77.3 us
    ppermute x22, starting transfers between devices, with_halo(): lax.ppermute(head, axis, [((i + 1) % count, i) for i in range(count)])  64.7 us
    conv_general_dilated x30, local copies, waits for them, and re-layouts, convolve(): lax.conv_general_dilated(padded, kernel, (1, 1), 'VALID', dimension_numbe...  51.4 us
    select_n x10, other arithmetic, close_rows(): return jnp.where(outside[:, None], jnp.zeros((), padded.dtype), padded)  33.3 us
    unnamed x54, local copies, waits for them, and re-layouts  23.1 us
    ppermute x22, waiting for transfers between devices, with_halo(): lax.ppermute(tail, axis, [(i, (i + 1) % count) for i in range(count)])  15.5 us
  transfers between devices with their start and end apart: 44, of which 12 were waited for; matrix products, arithmetic and copies ran while one was open for 10% of the time, Pallas kernels for 0%

commit v1 on v0

v1 whole, which is shorter than its diff:
```python
import functools

import jax
import jax.numpy as jnp
import numpy as np
from jax import lax
from jax.experimental import pallas as pl
from jax.experimental.pallas import tpu as pltpu
from jax.sharding import PartitionSpec as P

F32 = jnp.float32
BF16 = jnp.bfloat16
HALO = 12
SIDE = 16
CENTRE = 6.125
RADIUS = 5.875
VMEM = 60 * 1024 * 1024


def one_hots(rows, cols, sides):
    first = np.zeros((16, 96, 32), np.float32)
    last = np.zeros((16, 96, 32), np.float32)
    for s in range(16):
        jj, qr, qc = s // 4, s // 2 % 2, s % 2
        for dr in range(6):
            for x in range(16):
                a, b = dr - qr, x - 2 * jj - qc
                if 0 <= a < 5 and 0 <= b < 5:
                    first[s, dr * 16 + x, a * 5 + b] = 1
                    last[s, dr * 16 + x, (4 - a) * 5 + 4 - b] = 1
    force = np.zeros((4, 72, 32), np.float32)
    grad = np.zeros((4, 2, 72, 32), np.float32)
    for p in range(4):
        pr, pc = p // 2, p % 2
        for dr in range(3):
            for dc in range(3):
                for q in range(4):
                    qr, qc = q // 2, q % 2
                    a, b = 2 * dr + pr - qr, 2 * dc + pc - qc
                    if 0 <= a < 5 and 0 <= b < 5:
                        force[p, (dr * 3 + dc) * 8 + q, a * 5 + b] = 1
                        for ch in range(2):
                            grad[p, ch, (dr * 3 + dc) * 8 + ch * 4 + q, (4 - a) * 5 + 4 - b] = 1
    seen = np.zeros((128, 1024), np.float32)
    for s in range(16):
        jj, qr, qc = s // 4, s // 2 % 2, s % 2
        seen[96 + qr * 16 + 2 + 2 * jj + qc, s * 64 : s * 64 + 64] = 1
    return [jnp.asarray(t, BF16) for t in (first, last, force, grad, seen)]


def decimate(ext_rows, blocks):
    table = np.zeros((ext_rows, 768), np.float32)
    for dr in range(6):
        for i in range(blocks):
            table[2 * i + dr, dr * 128 + i] = 1
    return jnp.asarray(table, BF16)


def unfold_tables(rows, blocks, first_row, pairs, width, first_col):
    left = np.zeros((2 * rows, 256), np.float32)
    right = np.zeros((2, 2 * pairs, width), np.float32)
    for par in range(2):
        for qr in range(2):
            for i in range(blocks):
                row = 2 * i + qr + first_row
                if 0 <= row < rows:
                    left[par * rows + row, qr * 128 + par * 64 + i] = 1
        for qc in range(2):
            for jp in range(pairs):
                col = 4 * jp + 2 * par + qc + first_col
                if col < 128 + SIDE and col >= -SIDE:
                    right[par, qc * pairs + jp, col % width] = 1
    return jnp.asarray(left), jnp.asarray(right)


def mm(a, b, dims=((1,), (0,))):
    return lax.dot_general(a, b, (dims, ((), ())), preferred_element_type=F32)


def exact(a, b, dims=((1,), (0,))):
    return lax.dot_general(
        a, b, (dims, ((), ())), preferred_element_type=F32, precision=lax.Precision.HIGHEST
    )


def up(x, by):
    return x if by == 0 else pltpu.roll(x, x.shape[0] - by, axis=0)


def fold_middle(k_ref, out_ref, flip_ref):
    zero = jnp.zeros((64, 64), BF16)
    for dc in range(3):
        for dr in range(3):
            for p in range(4):
                pr, pc = p // 2, p % 2
                parts = []
                for q in range(4):
                    qr, qc = q // 2, q % 2
                    a, b = 2 * dr + pr - qr, 2 * dc + pc - qc
                    parts.append(k_ref[a * 5 + b] if 0 <= a < 5 and 0 <= b < 5 else zero)
                at = (dc * 3 + dr) * 256 + p * 64
                out_ref[at : at + 64, :] = jnp.concatenate(parts, axis=1)
    for tap in range(9):
        block = out_ref[tap * 256 : tap * 256 + 256, :].astype(F32)
        at = (8 - tap) * 256
        flip_ref[at : at + 256, :] = block.T.astype(BF16)


def weights_kernel(
    k_one, k_two, w_first, w_last, e_first, e_last, e_force, e_grad,
    m_one, m_one_t, m_two, m_two_t, r_first, r_last, t_force, t_grad,
):
    fold_middle(k_one, m_one, m_one_t)
    fold_middle(k_two, m_two, m_two_t)
    wf = w_first[...]
    wl = w_last[...]
    pad = jnp.zeros((7, 64), BF16)
    wf = [jnp.concatenate([wf[:, c * 64 : c * 64 + 64], pad], axis=0) for c in range(2)]
    wl = jnp.concatenate([wl, pad], axis=0)
    gap = jnp.zeros((32, 128), BF16)
    for s in range(0, 16, 2):
        cols = slice(s * 64, s * 64 + 128)
        for c in range(2):
            two = [mm(e_first[s + d], wf[c]).astype(BF16) for d in range(2)]
            r_first[c * 128 : c * 128 + 96, cols] = jnp.concatenate(two, axis=1)
            r_first[c * 128 + 96 : c * 128 + 128, cols] = gap
        two = [mm(e_last[s + d], wl).astype(BF16) for d in range(2)]
        r_last[0:96, cols] = jnp.concatenate(two, axis=1)
        r_last[96:128, cols] = gap
    force, grad = [], []
    for p in range(4):
        force.append(mm(e_force[p], wl))
        grad.append(mm(e_grad[p, 0], wf[0]) + mm(e_grad[p, 1], wf[1]))
    t_force[...] = jnp.concatenate(force, axis=1).astype(BF16)
    t_grad[...] = jnp.concatenate(grad, axis=1).astype(BF16)


def fold_weights(k_one, k_two, w_first, w_last, tables):
    big = jax.ShapeDtypeStruct((2304, 256), BF16)
    return pl.pallas_call(
        weights_kernel,
        name="fold_weights",
        out_shape=(
            big, big, big, big,
            jax.ShapeDtypeStruct((256, 1024), BF16),
            jax.ShapeDtypeStruct((128, 1024), BF16),
            jax.ShapeDtypeStruct((72, 256), BF16),
            jax.ShapeDtypeStruct((72, 256), BF16),
        ),
        compiler_params=pltpu.CompilerParams(vmem_limit_bytes=VMEM),
        cost_estimate=pl.CostEstimate(flops=1 << 24, bytes_accessed=1 << 23, transcendentals=0),
    )(k_one, k_two, w_first, w_last, *tables)


def thin_conv(table, slots, outs, flat_ref):
    count = slots.shape[0]
    for q in range(0, count, 4):
        take = min(4, count - q)
        x = slots[q : q + take].reshape(take * 64, 256)
        flat_ref[:, q * 64 : (q + take) * 64] = mm(table, x, ((1,), (1,)))
    span = (outs + 1) // 2 * 128
    total = None
    for dr in range(3):
        part = None
        for dc in range(3):
            tap = flat_ref[(dr * 3 + dc) * 8 : (dr * 3 + dc) * 8 + 8, dc * 64 : dc * 64 + span]
            part = tap if part is None else part + tap
        if dr:
            part = pltpu.roll(part, span - dr, axis=1)
        total = part if total is None else total + part
    return total


def unfold(image, base, pairs, rows, left, right, turn_ref):
    for jp in range(image.shape[1] // 128):
        turn_ref[jp * 8 : jp * 8 + 8, :] = image[:, jp * 128 : jp * 128 + 128]
    picks = []
    for qc in range(2):
        two = [turn_ref[pl.ds(base + qr * 2 + qc, pairs, stride=8), :] for qr in range(2)]
        picks.append(jnp.concatenate(two, axis=1))
    half = exact(left, jnp.concatenate(picks, axis=0), ((1,), (1,)))
    return exact(half[:rows], right[0]) + exact(half[rows:], right[1])


def tangent_kernel(
    own, rim, pick, seen, m_one, m_two, r_first, r_last, t_force, left, right,
    back_three, keep_two, keep_one, basis, gram,
    window, act_one, act_two, back_pre, mask_two, mask_three, tl_three, flat, turn,
):
    tall = own.shape[1]
    sel = pick[...]
    for c in range(6):
        for source, part in ((own, 0), (rim, 1)):
            image = source[c]
            if c == 4:
                image = image * source[5]
            turned_image = mm(image.astype(BF16), sel, ((0,), (0,)))
            if part == 0:
                window[c, SIDE : SIDE + 128, :] = turned_image
            else:
                window[c, SIDE + 128 : SIDE + 128 + SIDE, :] = turned_image[:SIDE]
                window[c, 0:SIDE, :] = turned_image[128 - SIDE :]

    act_two[72:74] = jnp.zeros((2, 80, 768), BF16)
    tl_three[:, 48:64] = jnp.zeros((72, 16, 256), BF16)

    def first_layer(m, _):
        views = [window[c, pl.ds(pl.multiple_of(m * 8, 8), 16), :] for c in range(6)]

        def stack(c):
            parts = [views[c][:, dr * 128 : dr * 128 + 128] for dr in range(6)]
            parts += [views[5][:, dr * 128 : dr * 128 + 128] for dr in (2, 3)]
            return jnp.concatenate(parts, axis=0).T[:48]

        slabs = [stack(c) for c in range(5)]
        base = jnp.concatenate(slabs[0:2], axis=1)
        incr = jnp.concatenate(slabs[2:4], axis=1)
        pre = mm(jnp.concatenate([base, incr], axis=0).astype(BF16), r_first[...])
        cells = seen[...]
        wet = mm(slabs[0].astype(BF16), cells)
        wet_two = mm(up(slabs[0], 1).astype(BF16), cells).astype(BF16)
        wet_three = mm(up(slabs[0], 2).astype(BF16), cells).astype(BF16)
        pre_back = mm(up(slabs[4], 2).astype(BF16), r_last[...])
        for jj in range(4):
            lanes = slice(jj * 256, jj * 256 + 256)
            a = m * 4 + jj
            slope = jnp.tanh(pre[0:48, lanes])
            mask = wet[:, lanes]
            keep = mask * (1.0 - slope * slope)
            act = mask * slope
            tangent = keep * pre[48:96, lanes]
            keep_one[a] = up(keep, 4)[0:40]
            for dr in range(3):
                both = jnp.concatenate([up(act, dr)[0:40], up(tangent, dr)[0:40]], axis=0)
                act_one[a, :, dr * 256 : dr * 256 + 256] = both.astype(BF16)
            mask_two[a] = wet_two[:, lanes]
            mask_three[a] = wet_three[:, lanes]
            back_pre[a] = pre_back[0:40, lanes]
        return 0

    lax.fori_loop(0, 19, first_layer, 0)

    def second_layer(q, _):
        b = q * 4
        taps = [act_one[pl.ds(b + 2 + dc, 4)].reshape(320, 768) for dc in range(3)]
        pre = mm(jnp.concatenate(taps, axis=1), m_one[...])
        for jj in range(4):
            slope = jnp.tanh(pre[jj * 80 : jj * 80 + 40])
            mask = mask_two[b + 3 + jj].astype(F32)[0:40]
            keep = mask * (1.0 - slope * slope)
            act = mask * slope
            tangent = keep * pre[jj * 80 + 40 : jj * 80 + 80]
            keep_two[b + jj] = up(keep, 2)
            for dr in range(3):
                both = jnp.concatenate([up(act, dr), up(tangent, dr)], axis=0)
                act_two[b + jj, :, dr * 256 : dr * 256 + 256] = both.astype(BF16)
        return 0

    lax.fori_loop(0, 18, second_layer, 0)

    def third_layer(q, _):
        t = q * 4
        taps = [act_two[pl.ds(t + dc, 4)].reshape(320, 768) for dc in range(3)]
        pre = mm(jnp.concatenate(taps, axis=1), m_two[...])
        rest = jnp.zeros((8, 256), F32)
        for jj in range(4):
            slope = jnp.tanh(pre[jj * 80 : jj * 80 + 40])
            mask = mask_three[t + 4 + jj].astype(F32)[0:40]
            keep = mask * (1.0 - slope * slope)
            tangent = keep * pre[jj * 80 + 40 : jj * 80 + 80]
            tl_three[t + jj, 0:48] = jnp.concatenate([tangent, rest], axis=0).astype(BF16)
            back = keep * back_pre[t + 4 + jj]
            back_three[t + jj] = jnp.concatenate([back, rest], axis=0).astype(BF16)
        return 0

    lax.fori_loop(0, 18, third_layer, 0)
    tl_three[70:72] = jnp.zeros((2, 64, 256), BF16)

    turn[...] = jnp.zeros(turn.shape, F32)
    image = thin_conv(t_force[...], tl_three, 68, flat)
    force = unfold(image, 0, 40, tall, left[...], right, turn)

    def wide(c):
        return jnp.concatenate([own[c], rim[c]], axis=1)

    mask, storage, source = wide(5), wide(6), wide(7)
    columns = mask.shape[1]
    east = mask * pltpu.roll(mask, columns - 1, axis=1)
    west = mask * pltpu.roll(mask, 1, axis=1)
    north = mask * pltpu.roll(mask, tall - 1, axis=0)
    south = mask * pltpu.roll(mask, 1, axis=0)

    def scaled(v):
        total = storage * v + east * (v - pltpu.roll(v, columns - 1, axis=1))
        total = total + west * (v - pltpu.roll(v, 1, axis=1))
        total = total + north * (v - pltpu.roll(v, tall - 1, axis=0))
        total = total + south * (v - pltpu.roll(v, 1, axis=0))
        return (total - CENTRE * v) * (1.0 / RADIUS)

    v0 = source + mask * force
    v1 = scaled(v0)
    v2 = 2.0 * scaled(v1) - v0
    v3 = 2.0 * scaled(v2) - v1
    inner = [v[HALO : tall - HALO, 0:128] for v in (v0, v1, v2, v3)]
    for k in range(4):
        basis[k] = inner[k]
    lane = lax.broadcasted_iota(jnp.int32, (8, 128), 1)
    sums = jnp.zeros((8, 128), F32)
    at = 0
    for i in range(4):
        for j in range(i, 4):
            prod = jnp.sum(inner[i] * inner[j], axis=0, keepdims=True)
            value = jnp.sum(prod, axis=1, keepdims=True)
            sums = jnp.where(lane == at, value, sums)
            at += 1
    gram[...] = sums


def tangent_pass(own, rim, pick, seen, mats, left, right):
    m_one, m_two, r_first, r_last, t_force = mats
    tall = own.shape[1]
    rows = tall - 2 * HALO
    return pl.pallas_call(
        tangent_kernel,
        name="tangent_pass",
        out_shape=(
            jax.ShapeDtypeStruct((72, 48, 256), BF16),
            jax.ShapeDtypeStruct((72, 40, 256), F32),
            jax.ShapeDtypeStruct((76, 40, 256), F32),
            jax.ShapeDtypeStruct((4, rows, 128), F32),
            jax.ShapeDtypeStruct((8, 128), F32),
        ),
        scratch_shapes=[
            pltpu.VMEM((6, 128 + 2 * SIDE, 768), F32),
            pltpu.VMEM((76, 80, 768), BF16),
            pltpu.VMEM((74, 80, 768), BF16),
            pltpu.VMEM((76, 40, 256), F32),
            pltpu.VMEM((76, 48, 256), BF16),
            pltpu.VMEM((76, 48, 256), BF16),
            pltpu.VMEM((72, 64, 256), BF16),
            pltpu.VMEM((72, 72 * 64), F32),
            pltpu.VMEM((320, 128), F32),
        ],
        compiler_params=pltpu.CompilerParams(vmem_limit_bytes=VMEM),
        cost_estimate=pl.CostEstimate(flops=1 << 33, bytes_accessed=1 << 24, transcendentals=1 << 21),
    )(own, rim, pick, seen, m_one, m_two, r_first, r_last, t_force, left, right)


def adjoint_kernel(
    back_three, keep_two, keep_one, m_one_t, m_two_t, t_grad, left, right,
    grad, three, two, one, flat, turn,
):
    def spread(s, _):
        x0 = back_three[s].astype(F32)[0:40]
        x1 = back_three[s + 32].astype(F32)[0:40]
        for dr in range(3):
            both = jnp.concatenate([up(x0, dr), up(x1, dr)], axis=0)
            three[s, :, dr * 256 : dr * 256 + 256] = both.astype(BF16)
        return 0

    lax.fori_loop(0, 38, spread, 0, unroll=2)

    def second_layer(q, _):
        s = q * 4
        taps = [three[pl.ds(s + dc, 4)].reshape(320, 768) for dc in range(3)]
        pre = mm(jnp.concatenate(taps, axis=1), m_two_t[...])
        for jj in range(4):
            x0 = pre[jj * 80 : jj * 80 + 40] * keep_two[s + 2 + jj]
            x1 = pre[jj * 80 + 40 : jj * 80 + 80] * keep_two[s + 34 + jj]
            for dr in range(3):
                both = jnp.concatenate([up(x0, dr), up(x1, dr)], axis=0)
                two[s + jj, :, dr * 256 : dr * 256 + 256] = both.astype(BF16)
        return 0

    lax.fori_loop(0, 9, second_layer, 0)
    one[:, 48:64] = jnp.zeros((66, 16, 256), BF16)
    rest = jnp.zeros((8, 256), F32)

    def first_layer(s, count):
        taps = [two[pl.ds(s + dc, count)].reshape(count * 80, 768) for dc in range(3)]
        pre = mm(jnp.concatenate(taps, axis=1), m_one_t[...])
        for jj in range(count):
            x0 = pre[jj * 80 : jj * 80 + 40] * keep_one[s + 6 + jj]
            x1 = pre[jj * 80 + 40 : jj * 80 + 80] * keep_one[s + 38 + jj]
            one[s + jj, 0:48] = jnp.concatenate([x0, rest], axis=0).astype(BF16)
            one[s + 32 + jj, 0:48] = jnp.concatenate([x1, rest], axis=0).astype(BF16)

    def body(q, _):
        first_layer(q * 4, 4)
        return 0

    lax.fori_loop(0, 8, body, 0)
    first_layer(32, 2)

    image = thin_conv(t_grad[...], one, 64, flat)
    rows = grad.shape[1]
    for ch in range(2):
        grad[ch] = unfold(image, ch * 4, 32, rows, left[...], right, turn)


def adjoint_pass(back_three, keep_two, keep_one, mats, left, right):
    m_one_t, m_two_t, t_grad = mats
    return pl.pallas_call(
        adjoint_kernel,
        name="adjoint_pass",
        out_shape=jax.ShapeDtypeStruct((2, left.shape[0] // 2, 128), F32),
        scratch_shapes=[
            pltpu.VMEM((38, 80, 768), BF16),
            pltpu.VMEM((36, 80, 768), BF16),
            pltpu.VMEM((66, 64, 256), BF16),
            pltpu.VMEM((72, 66 * 64), F32),
            pltpu.VMEM((256, 128), F32),
        ],
        compiler_params=pltpu.CompilerParams(vmem_limit_bytes=VMEM),
        cost_estimate=pl.CostEstimate(flops=1 << 33, bytes_accessed=1 << 24, transcendentals=0),
    )(back_three, keep_two, keep_one, m_one_t, m_two_t, t_grad, left, right)


def combine_kernel(basis, gram, surface, residual):
    sums = gram[0:1, :]
    g = {}
    at = 0
    for i in range(4):
        for j in range(i, 4):
            g[i, j] = g[j, i] = sums[:, at : at + 1]
            at += 1

    def inner(a, b):
        total = None
        for i, ai in enumerate(a):
            for j, bj in enumerate(b):
                if ai is not None and bj is not None:
                    term = ai * bj * g[i, j]
                    total = term if total is None else total + term
        return total

    def add(a, b, scale):
        out = []
        for ai, bi in zip(a, b):
            if bi is None:
                out.append(ai)
            else:
                out.append(scale * bi if ai is None else ai + scale * bi)
        return out

    def operate(p):
        out = [None if x is None else CENTRE * x for x in p]
        if p[0] is not None:
            out = add(out, [None, p[0], None, None], RADIUS)
        if p[1] is not None:
            out = add(out, [p[1], None, p[1], None], 0.5 * RADIUS)
        if p[2] is not None:
            out = add(out, [None, p[2], None, p[2]], 0.5 * RADIUS)
        return out

    unit = jnp.ones((1, 1), F32)
    r = [unit, None, None, None]
    p = [unit, None, None, None]
    x = [None] * 4
    norm = g[0, 0]
    for step in range(3):
        image = operate(p)
        alpha = norm / inner(p, image)
        x = add(x, p, alpha)
        r = add(r, image, -alpha)
        if step < 2:
            new = inner(r, r)
            p = add(r, p, new / norm)
            norm = new
    surface[...] = x[0] * basis[0] + x[1] * basis[1] + x[2] * basis[2]
    residual[...] = r[0] * basis[0] + r[1] * basis[1] + r[2] * basis[2] + r[3] * basis[3]


def combine(basis, gram):
    shape = jax.ShapeDtypeStruct(basis.shape[1:], F32)
    return pl.pallas_call(combine_kernel, name="combine", out_shape=(shape, shape))(basis, gram)


def everywhere(x):
    for axis in ("gy", "gx"):
        count = lax.axis_size(axis)
        if count & (count - 1):
            x = lax.psum(x, axis)
            continue
        step = 1
        while step < count:
            x = x + lax.ppermute(x, axis, [(i, i ^ step) for i in range(count)])
            step *= 2
    return x


def shards(
    base_state,
    increment,
    cotangent,
    land_sea,
    storage,
    source,
    w_first,
    w_middle_one,
    w_middle_two,
    w_last,
):
    rows, cols = land_sea.shape
    tall = rows + 2 * HALO
    gx, gy = lax.axis_size("gx"), lax.axis_size("gy")
    own = jnp.concatenate(
        [
            base_state.astype(F32),
            increment.astype(F32),
            cotangent.astype(F32)[None],
            land_sea.astype(F32)[None],
            storage[None],
            source[None],
        ],
        axis=0,
    )
    above = lax.ppermute(own[:, rows - HALO :], "gy", [(i, i + 1) for i in range(gy - 1)])
    below = lax.ppermute(own[:, :HALO], "gy", [(i + 1, i) for i in range(gy - 1)])
    own = jnp.concatenate([above, own, below], axis=1)
    west = lax.ppermute(own[:, :, cols - SIDE :], "gx", [(i, (i + 1) % gx) for i in range(gx)])
    east = lax.ppermute(own[:, :, :SIDE], "gx", [((i + 1) % gx, i) for i in range(gx)])
    gap = jnp.zeros((8, tall, 128 - 2 * SIDE), F32)
    rim = jnp.concatenate([east, gap, west], axis=2)

    e_first, e_last, e_force, e_grad, seen = one_hots(rows, cols, SIDE)
    m_one, m_one_t, m_two, m_two_t, r_first, r_last, t_force, t_grad = fold_weights(
        w_middle_one.reshape(25, 64, 64),
        w_middle_two.reshape(25, 64, 64),
        w_first,
        w_last,
        (e_first, e_last, e_force, e_grad),
    )
    left, right = unfold_tables(tall, 36, 8, 40, 256, -4)
    back_three, keep_two, keep_one, basis, gram = tangent_pass(
        own, rim, decimate(tall, 42), seen, (m_one, m_two, r_first, r_last, t_force), left, right
    )
    gram = everywhere(gram)
    left, right = unfold_tables(rows, 32, 0, 32, 128, 0)
    grad = adjoint_pass(back_three, keep_two, keep_one, (m_one_t, m_two_t, t_grad), left, right)
    surface, residual = combine(basis, gram)
    return (grad, surface, residual)


def solution(mesh):
    placed = (
        P(None, "gy", "gx"),
        P(None, "gy", "gx"),
        P("gy", "gx"),
        P("gy", "gx"),
        P("gy", "gx"),
        P("gy", "gx"),
        P(),
        P(),
        P(),
        P(),
    )
    return jax.shard_map(
        shards,
        mesh=mesh,
        in_specs=placed,
        out_specs=(P(None, "gy", "gx"), P("gy", "gx"), P("gy", "gx")),
        check_vma=False,
    )
```

time: 700 us -> 103 us (0.15); the launches traced: 692 us -> 102 us
  matrix products: 229 us -> 0 us
  blocking collectives: 199 us -> 0 us
  local copies, waits for them, and re-layouts: 89.9 us -> 4.12 us
  other arithmetic: 73.7 us -> 5.24 us
  starting transfers between devices: 74 us -> 13.7 us
  Pallas kernels: 0 us -> 58.5 us
  between operations: 8.55 us -> 0.7 us
    conv_general_dilated x8 -> x0, matrix products: 229 us -> none  [convolve(): lax.conv_general_dilated(padded, kernel, (1, 1), 'VALID', dimension_numbe...]
    psum x5 -> x0, blocking collectives: 199 us -> none  [the longest x3 122 us: squares(): return lax.psum(jnp.sum(residual * residual), ('gx', 'gy'))]
    ppermute x44 -> x9, starting transfers between devices: 74 us -> 13.7 us  [the longest x5 5.31 us: everywhere(): x = x + lax.ppermute(x, axis, [(i, i ^ step) for i in range(count)])]
    pallas_call x0 -> x4, Pallas kernels: none -> 58.5 us  [the longest x1 35.1 us: tangent_pass(): pl.pallas_call(tangent_kernel, name='tangent_pass', out_shape=(jax.ShapeD...]
    conv_general_dilated x30 -> x0, local copies, waits for them, and re-layouts: 51.4 us -> none  [convolve(): lax.conv_general_dilated(padded, kernel, (1, 1), 'VALID', dimension_numbe...]
    select_n x10 -> x0, other arithmetic: 33.3 us -> none  [close_rows(): return jnp.where(outside[:, None], jnp.zeros((), padded.dtype), padded)]
    convert_element_type x7 -> x0, other arithmetic: 23.5 us -> none  [the longest x1 11.2 us: shards(): act_two = (mask * slope_two).astype(jnp.bfloat16)]
    unnamed x54 -> x7, local copies, waits for them, and re-layouts: 23.1 us -> 0.77 us
  transfers between devices with their start and end apart: 44 -> 9, of which waited for: 12 -> 6; matrix products, arithmetic and copies ran while one was open for 10% -> 2% of each run, Pallas kernels for 0% -> 21%
where the time goes in v1:
time: 103 us; the launch traced here: 102 us
  Pallas kernels  58.5 us (57%)
  waiting for transfers between devices  20.2 us (20%)
  starting transfers between devices  13.7 us (13%)
  other arithmetic  5.24 us (5%)
  local copies, waits for them, and re-layouts  4.12 us (4%)
    pallas_call x1, Pallas kernels, tangent_pass(): pl.pallas_call(tangent_kernel, name='tangent_pass', out_shape=(jax.ShapeD...  35.1 us
    pallas_call x1, Pallas kernels, adjoint_pass(): pl.pallas_call(adjoint_kernel, name='adjoint_pass', out_shape=jax.ShapeDt...  16.9 us
    ppermute x5, waiting for transfers between devices, everywhere(): x = x + lax.ppermute(x, axis, [(i, i ^ step) for i in range(count)])  9.12 us
    ppermute x1, waiting for transfers between devices, shards(): lax.ppermute(own[:, :, cols - SIDE:], 'gx', [(i, (i + 1) % gx) for i in r...  7.13 us
    ppermute x5, starting transfers between devices, everywhere(): x = x + lax.ppermute(x, axis, [(i, i ^ step) for i in range(count)])  5.31 us
    pallas_call x1, Pallas kernels, fold_weights(): pl.pallas_call(weights_kernel, name='fold_weights', out_shape=(big, big,...  4.74 us
    ppermute x1, starting transfers between devices, shards(): lax.ppermute(own[:, :, :SIDE], 'gx', [((i + 1) % gx, i) for i in range(gx)])  4.61 us
    ppermute x1, waiting for transfers between devices, shards(): lax.ppermute(own[:, :HALO], 'gy', [(i + 1, i) for i in range(gy - 1)])  3.94 us
  transfers between devices with their start and end apart: 9, of which 6 were waited for; matrix products, arithmetic and copies ran while one was open for 2% of the time, Pallas kernels for 21%

profile of v1, /device:TPU:0, one launch (start us, length us, event | category | flops | bytes accessed | tf_op | source)
XLA Modules:
  0.0 102.4 jit_solution(3054997366691358458)
XLA Ops:
  0.6 0.8 convert_dynamic-update-slice_fusion.1
  1.4 0.8 convert_dynamic-update-slice_fusion
  2.2 0.7 convert_dynamic-update-slice_fusion.2
  2.9 0.8 bitcast_dynamic-update-slice_fusion.2
  3.6 0.8 bitcast_dynamic-update-slice_fusion.1
  4.4 0.8 bitcast_dynamic-update-slice_fusion
  5.2 0.0 copy-start.1
  5.2 2.5 %collective-permute-start = (f32[8,12,128]{2,1,0:T(8,128)S(1)}, f32[8,12,128]{2,1,0:T(8,128)S(1)}, u32[]{:S(2)}, u32[]{:S(2)}) collective-permute-start(f32[8,12,128]{2,1,0:T(8,128)S(1)} %get-tuple-element.35), channel_id=1, source_target_pairs={{0,1},{1,2},{2,3},{4,5},{5,6},{6,7},{8,9},{9,10},{10,11},{12,13},{... | collective-permute-start | bytes 147464 | tf_op jit(solution)/shard_map/ppermute | solution.py:518
  7.7 1.3 %collective-permute-start.1 = (f32[8,12,128]{2,1,0:T(8,128)S(1)}, f32[8,12,128]{2,1,0:T(8,128)S(1)}, u32[]{:S(2)}, u32[]{:S(2)}) collective-permute-start(f32[8,12,128]{2,1,0:T(8,128)S(1)} %get-tuple-element.36), channel_id=1, source_target_pairs={{1,0},{2,1},{3,2},{5,4},{6,5},{7,6},{9,8},{10,9},{11,10},{13,12},{... | collective-permute-start | bytes 147464 | tf_op jit(solution)/shard_map/ppermute | solution.py:519
  9.0 0.0 collective-permute-done
  9.0 3.9 %collective-permute-done.1 = f32[8,12,128]{2,1,0:T(8,128)S(1)} collective-permute-done((f32[8,12,128]{2,1,0:T(8,128)S(1)}, f32[8,12,128]{2,1,0:T(8,128)S(1)}, u32[]{:S(2)}, u32[]{:S(2)}) %collective-permute-start.1) | collective-permute-done | bytes 49184 | tf_op jit(solution)/shard_map/ppermute | solution.py:519
  13.0 0.0 copy-start
  13.0 0.0 copy-start.2
  13.0 0.2 fusion
  13.2 4.6 %collective-permute-start.2 = (f32[8,88,16]{2,1,0:T(8,128)S(1)}, f32[8,88,16]{2,1,0:T(8,128)S(1)}, u32[]{:S(2)}, u32[]{:S(2)}) collective-permute-start(f32[8,88,16]{2,1,0:T(8,128)S(1)} %get-tuple-element.33), channel_id=1, source_target_pairs={{4,0},{8,4},{12,8},{16,12},{20,16},{24,20},{28,24},{0,28},{5,1},{9... | collective-permute-start | bytes 135176 | tf_op jit(solution)/shard_map/ppermute | solution.py:522
  17.8 0.0 collective-permute-start.3
  17.8 0.0 copy-done.1
  17.8 1.2 %reshape.12.k_one = bf16[25,64,64]{2,1,0:T(8,128)(2,1)} reshape(bf16[25,4096]{1,0:T(8,128)(2,1)S(1)} %copy-done.1) | data formatting | bytes 409600 | tf_op jit(solution)/shard_map/reshape | solution.py:528
  18.9 0.0 copy-done.2
  19.0 1.2 %reshape.13.k_two = bf16[25,64,64]{2,1,0:T(8,128)(2,1)} reshape(bf16[25,4096]{1,0:T(8,128)(2,1)S(1)} %copy-done.2) | data formatting | bytes 409600 | tf_op jit(solution)/shard_map/reshape | solution.py:529
  20.1 0.0 copy-done
  20.1 0.1 pad.1.clone
  20.2 4.7 %fold_weights.1 = (bf16[2304,256]{1,0:T(8,128)(2,1)}, bf16[2304,256]{1,0:T(8,128)(2,1)}, bf16[2304,256]{1,0:T(8,128)(2,1)}, bf16[2304,256]{1,0:T(8,128)(2,1)}, b...) custom-call(bf16[25,64,64]{2,1,0:T(8,128)(2,1)} %reshape.12.k_one, ...), custom_call_target="tpu_custom_call" | custom-call | flops 16777216 | bytes 8388608 | tf_op jit(solution)/shard_map/fold_weights/pallas_call | solution.py:140
  24.9 0.0 collective-permute-done.2
  24.9 7.1 %collective-permute-done.3 = f32[8,88,16]{2,1,0:T(8,128)S(1)} collective-permute-done((f32[8,88,16]{2,1,0:T(8,128)S(1)}, f32[8,88,16]{2,1,0:T(8,128)S(1)}, u32[]{:S(2)}, u32[]{:S(2)}) %collective-permute-start.3) | collective-permute-done | bytes 45088 | tf_op jit(solution)/shard_map/ppermute | solution.py:521
  32.1 0.9 pad_maximum_fusion.1.rim
  33.0 35.1 %tangent_pass.1 = (bf16[72,48,256]{2,1,0:T(8,128)(2,1)}, f32[72,40,256]{2,1,0:T(8,128)}, f32[76,40,256]{2,1,0:T(8,128)}, f32[4,64,128]{2,1,0:T(8,128)}, f32[8,128]{1,0:T(8,128)}) custom-call(f32[8,88,128]{2,1,0:T(8,128)} %copy-done, f32[8,88,128]{2,1,0:T(8,128)} %pad_maximum_fusion.1.rim, bf16[88,768]{1,0:T(8,128)(2,1)} %constant.29.clone.pick, ...), custom_call_target="tpu_custom_call" | custom-call | flops 8589934592 | bytes 16777216 | tf_op jit(solution)/shard_map/tangent_pass/pallas_call | solution.py:323
  68.1 0.3 collective-permute-start.4
  68.4 1.1 %collective-permute-done.4 = f32[8,128]{1,0:T(8,128)S(1)} collective-permute-done((f32[8,128]{1,0:T(8,128)}, f32[8,128]{1,0:T(8,128)S(1)}, u32[]{:S(2)}, u32[]{:S(2)}) %collective-permute-start.4) | collective-permute-done | bytes 4128 | tf_op jit(solution)/shard_map/ppermute | solution.py:487
  69.5 0.7 add.15
  70.2 0.0 collective-permute-start.5
  70.2 3.6 %collective-permute-done.5 = f32[8,128]{1,0:T(8,128)S(1)} collective-permute-done((f32[8,128]{1,0:T(8,128)S(1)}, f32[8,128]{1,0:T(8,128)S(1)}, u32[]{:S(2)}, u32[]{:S(2)}) %collective-permute-start.5) | collective-permute-done | bytes 4128 | tf_op jit(solution)/shard_map/ppermute | solution.py:487
  73.8 2.5 %collective-permute-start.6 = (f32[8,128]{1,0:T(8,128)S(1)}, f32[8,128]{1,0:T(8,128)S(1)}, u32[]{:S(2)}, u32[]{:S(2)}) collective-permute-start(f32[8,128]{1,0:T(8,128)S(1)} %add.16), channel_id=1, source_target_pairs={{0,4},{4,0},{8,12},{12,8},{16,20},{20,16},{24,28},{28,24},{1,5},{5... | collective-permute-start | bytes 12296 | tf_op jit(solution)/shard_map/ppermute | solution.py:487
  76.3 1.6 %collective-permute-done.6 = f32[8,128]{1,0:T(8,128)S(1)} collective-permute-done((f32[8,128]{1,0:T(8,128)S(1)}, f32[8,128]{1,0:T(8,128)S(1)}, u32[]{:S(2)}, u32[]{:S(2)}) %collective-permute-start.6) | collective-permute-done | bytes 4128 | tf_op jit(solution)/shard_map/ppermute | solution.py:487
  77.8 0.8 collective-permute-start.7
  78.6 2.8 %collective-permute-done.7 = f32[8,128]{1,0:T(8,128)S(1)} collective-permute-done((f32[8,128]{1,0:T(8,128)S(1)}, f32[8,128]{1,0:T(8,128)S(1)}, u32[]{:S(2)}, u32[]{:S(2)}) %collective-permute-start.7) | collective-permute-done | bytes 4128 | tf_op jit(solution)/shard_map/ppermute | solution.py:487
  81.5 1.8 %collective-permute-start.8 = (f32[8,128]{1,0:T(8,128)S(1)}, f32[8,128]{1,0:T(8,128)S(1)}, u32[]{:S(2)}, u32[]{:S(2)}) collective-permute-start(f32[8,128]{1,0:T(8,128)S(1)} %add.18), channel_id=1, source_target_pairs={{0,16},{4,20},{8,24},{12,28},{16,0},{20,4},{24,8},{28,12},{1,17},{... | collective-permute-start | bytes 12296 | tf_op jit(solution)/shard_map/ppermute | solution.py:487
  83.2 16.9 %adjoint_pass.1 = f32[2,64,128]{2,1,0:T(8,128)} custom-call(bf16[72,48,256]{2,1,0:T(8,128)(2,1)} %get-tuple-element.23.back_three, f32[72,40,256]{2,1,0:T(8,128)} %get-tuple-element.24.keep_two, f32[76,40,256]{2,1,0:T(8,128)} %get-tuple-element.25.keep_one, bf16[2304,256]{1,0:T(8,128)(2,1)} %get-tuple-element.26.m_one_t, ...), custom_call_target="tpu_custom_call" | custom-call | flops 8589934592 | bytes 16777216 | tf_op jit(solution)/shard_map/adjoint_pass/pallas_call | solution.py:403
  100.1 0.0 collective-permute-done.8
  100.1 0.6 add.19.gram
  100.7 1.7 %combine.1 = (f32[64,128]{1,0:T(8,128)}, f32[64,128]{1,0:T(8,128)}) custom-call(f32[4,64,128]{2,1,0:T(8,128)} %get-tuple-element.29.basis, f32[8,128]{1,0:T(8,128)} %add.19.gram), custom_call_target="tpu_custom_call" | custom-call | tf_op jit(solution)/shard_map/combine/pallas_call | solution.py:476
  (6 shorter events, 0.1 us)
Async XLA Ops:
  5.2 12.6 %copy-start.1 = (bf16[25,4096]{1,0:T(8,128)(2,1)S(1)}, bf16[25,4096]{1,0:T(8,128)(2,1)}, u32[]{:S(2)}) copy-start(bf16[25,4096]{1,0:T(8,128)(2,1)} %param.27) | copy-start | bytes 614404
  5.2 3.8 %collective-permute-start = (f32[8,12,128]{2,1,0:T(8,128)S(1)}, f32[8,12,128]{2,1,0:T(8,128)S(1)}, u32[]{:S(2)}, u32[]{:S(2)}) collective-permute-start(f32[8,12,128]{2,1,0:T(8,128)S(1)} %get-tuple-element.35), channel_id=1, source_target_pairs={{0,1},{1,2},{2,3},{4,5},{5,6},{6,7},{8,9},{9,10},{10,11},{12,13},{... | collective-permute-start | bytes 147464 | tf_op jit(solution)/shard_map/ppermute | solution.py:518
  7.7 5.3 %collective-permute-start.1 = (f32[8,12,128]{2,1,0:T(8,128)S(1)}, f32[8,12,128]{2,1,0:T(8,128)S(1)}, u32[]{:S(2)}, u32[]{:S(2)}) collective-permute-start(f32[8,12,128]{2,1,0:T(8,128)S(1)} %get-tuple-element.36), channel_id=1, source_target_pairs={{1,0},{2,1},{3,2},{5,4},{6,5},{7,6},{9,8},{10,9},{11,10},{13,12},{... | collective-permute-start | bytes 147464 | tf_op jit(solution)/shard_map/ppermute | solution.py:519
  13.0 7.1 %copy-start = (f32[8,88,128]{2,1,0:T(8,128)}, f32[8,88,128]{2,1,0:T(8,128)S(1)}, u32[]{:S(2)}) copy-start(f32[8,88,128]{2,1,0:T(8,128)S(1)} %pad_maximum_fusion.own) | copy-start | bytes 1081348
  13.0 6.0 %copy-start.2 = (bf16[25,4096]{1,0:T(8,128)(2,1)S(1)}, bf16[25,4096]{1,0:T(8,128)(2,1)}, u32[]{:S(2)}) copy-start(bf16[25,4096]{1,0:T(8,128)(2,1)} %param.28) | copy-start | bytes 614404
  13.2 11.8 %collective-permute-start.2 = (f32[8,88,16]{2,1,0:T(8,128)S(1)}, f32[8,88,16]{2,1,0:T(8,128)S(1)}, u32[]{:S(2)}, u32[]{:S(2)}) collective-permute-start(f32[8,88,16]{2,1,0:T(8,128)S(1)} %get-tuple-element.33), channel_id=1, source_target_pairs={{4,0},{8,4},{12,8},{16,12},{20,16},{24,20},{28,24},{0,28},{5,1},{9... | collective-permute-start | bytes 135176 | tf_op jit(solution)/shard_map/ppermute | solution.py:522
  17.8 14.3 %collective-permute-start.3 = (f32[8,88,16]{2,1,0:T(8,128)S(1)}, f32[8,88,16]{2,1,0:T(8,128)S(1)}, u32[]{:S(2)}, u32[]{:S(2)}) collective-permute-start(f32[8,88,16]{2,1,0:T(8,128)S(1)} %get-tuple-element.34), channel_id=1, source_target_pairs={{0,4},{4,8},{8,12},{12,16},{16,20},{20,24},{24,28},{28,0},{1,5},{5... | collective-permute-start | bytes 135176 | tf_op jit(solution)/shard_map/ppermute | solution.py:521
  68.1 1.4 %collective-permute-start.4 = (f32[8,128]{1,0:T(8,128)}, f32[8,128]{1,0:T(8,128)S(1)}, u32[]{:S(2)}, u32[]{:S(2)}) collective-permute-start(f32[8,128]{1,0:T(8,128)} %get-tuple-element.30), channel_id=1, source_target_pairs={{0,1},{1,0},{2,3},{3,2},{4,5},{5,4},{6,7},{7,6},{8,9},{9,8},{10,11... | collective-permute-start | bytes 12296 | tf_op jit(solution)/shard_map/ppermute | solution.py:487
  70.2 3.6 %collective-permute-start.5 = (f32[8,128]{1,0:T(8,128)S(1)}, f32[8,128]{1,0:T(8,128)S(1)}, u32[]{:S(2)}, u32[]{:S(2)}) collective-permute-start(f32[8,128]{1,0:T(8,128)S(1)} %add.15), channel_id=1, source_target_pairs={{0,2},{1,3},{2,0},{3,1},{4,6},{5,7},{6,4},{7,5},{8,10},{9,11},{10,... | collective-permute-start | bytes 12296 | tf_op jit(solution)/shard_map/ppermute | solution.py:487
  73.8 4.1 %collective-permute-start.6 = (f32[8,128]{1,0:T(8,128)S(1)}, f32[8,128]{1,0:T(8,128)S(1)}, u32[]{:S(2)}, u32[]{:S(2)}) collective-permute-start(f32[8,128]{1,0:T(8,128)S(1)} %add.16), channel_id=1, source_target_pairs={{0,4},{4,0},{8,12},{12,8},{16,20},{20,16},{24,28},{28,24},{1,5},{5... | collective-permute-start | bytes 12296 | tf_op jit(solution)/shard_map/ppermute | solution.py:487
  77.8 3.6 %collective-permute-start.7 = (f32[8,128]{1,0:T(8,128)S(1)}, f32[8,128]{1,0:T(8,128)S(1)}, u32[]{:S(2)}, u32[]{:S(2)}) collective-permute-start(f32[8,128]{1,0:T(8,128)S(1)} %add.17), channel_id=1, source_target_pairs={{0,8},{4,12},{8,0},{12,4},{16,24},{20,28},{24,16},{28,20},{1,9},{5... | collective-permute-start | bytes 12296 | tf_op jit(solution)/shard_map/ppermute | solution.py:487
  81.5 18.6 %collective-permute-start.8 = (f32[8,128]{1,0:T(8,128)S(1)}, f32[8,128]{1,0:T(8,128)S(1)}, u32[]{:S(2)}, u32[]{:S(2)}) collective-permute-start(f32[8,128]{1,0:T(8,128)S(1)} %add.18), channel_id=1, source_target_pairs={{0,16},{4,20},{8,24},{12,28},{16,0},{20,4},{24,8},{28,12},{1,17},{... | collective-permute-start | bytes 12296 | tf_op jit(solution)/shard_map/ppermute | solution.py:487

commit v2 on v1

v2 whole, which is shorter than its diff:
```python
import functools

import jax
import jax.numpy as jnp
import numpy as np
from jax import lax
from jax.experimental import pallas as pl
from jax.experimental.pallas import tpu as pltpu
from jax.sharding import PartitionSpec as P

F32 = jnp.float32
BF16 = jnp.bfloat16
HALO = 16
CENTRE = 6.125
RADIUS = 5.875
VMEM = 60 * 1024 * 1024
ANY = pl.BlockSpec(memory_space=pl.ANY)
HERE = pl.BlockSpec(memory_space=pltpu.VMEM)


def one_hots():
    first = np.zeros((16, 96, 32), np.float32)
    last = np.zeros((16, 96, 32), np.float32)
    for s in range(16):
        jj, qr, qc = s // 4, s // 2 % 2, s % 2
        for dr in range(6):
            for x in range(16):
                a, b = dr - qr, x - 2 * jj - qc
                if 0 <= a < 5 and 0 <= b < 5:
                    first[s, dr * 16 + x, a * 5 + b] = 1
                    last[s, dr * 16 + x, (4 - a) * 5 + 4 - b] = 1
    force = np.zeros((4, 72, 32), np.float32)
    grad = np.zeros((4, 2, 72, 32), np.float32)
    for p in range(4):
        pr, pc = p // 2, p % 2
        for dr in range(3):
            for dc in range(3):
                for q in range(4):
                    qr, qc = q // 2, q % 2
                    a, b = 2 * dr + pr - qr, 2 * dc + pc - qc
                    if 0 <= a < 5 and 0 <= b < 5:
                        force[p, (dr * 3 + dc) * 8 + q, a * 5 + b] = 1
                        for ch in range(2):
                            grad[p, ch, (dr * 3 + dc) * 8 + ch * 4 + q, (4 - a) * 5 + 4 - b] = 1
    seen = np.zeros((128, 1024), np.float32)
    for s in range(16):
        jj, qr, qc = s // 4, s // 2 % 2, s % 2
        seen[96 + qr * 16 + 2 + 2 * jj + qc, s * 64 : s * 64 + 64] = 1
    return [jnp.asarray(t, BF16) for t in (first, last, force, grad, seen)]


def decimate():
    table = np.zeros((128, 768), np.float32)
    for dr in range(6):
        for i in range(42):
            table[2 * i + dr + 4, dr * 128 + i] = 1
    return jnp.asarray(table, BF16)


def unfold_tables(rows, blocks, first_row, pairs, width, first_col):
    left = np.zeros((2 * rows, 256), np.float32)
    right = np.zeros((2, 2 * pairs, width), np.float32)
    for par in range(2):
        for qr in range(2):
            for i in range(blocks):
                row = 2 * i + qr + first_row
                if 0 <= row < rows:
                    left[par * rows + row, qr * 128 + par * 64 + i] = 1
        for qc in range(2):
            for jp in range(pairs):
                col = 4 * jp + 2 * par + qc + first_col
                if -HALO <= col < 128 + HALO:
                    right[par, qc * pairs + jp, col % width] = 1
    return jnp.asarray(left), jnp.asarray(right)


def mm(a, b, dims=((1,), (0,))):
    return lax.dot_general(a, b, (dims, ((), ())), preferred_element_type=F32)


def exact(a, b, dims=((1,), (0,))):
    return lax.dot_general(
        a, b, (dims, ((), ())), preferred_element_type=F32, precision=lax.Precision.HIGHEST
    )


def up(x, by):
    return x if by == 0 else pltpu.roll(x, x.shape[0] - by, axis=0)


def unpack_taps(raw, stage, taps):
    for i in range(32):
        stage[i * 32 : i * 32 + 25, :] = raw[:, i * 128 : i * 128 + 128].astype(F32)
    for t in range(25):
        pairs = stage[pl.ds(t, 32, stride=32), :]
        taps[t, pl.ds(0, 32, stride=2), :] = pairs[:, 0:64]
        taps[t, pl.ds(1, 32, stride=2), :] = pairs[:, 64:128]


def fold_middle(taps, out_ref):
    zero = jnp.zeros((64, 64), F32)
    for dc in range(3):
        for dr in range(3):
            for p in range(4):
                pr, pc = p // 2, p % 2
                parts = []
                for q in range(4):
                    qr, qc = q // 2, q % 2
                    a, b = 2 * dr + pr - qr, 2 * dc + pc - qc
                    parts.append(taps[a * 5 + b] if 0 <= a < 5 and 0 <= b < 5 else zero)
                at = (dc * 3 + dr) * 256 + p * 64
                out_ref[at : at + 64, :] = jnp.concatenate(parts, axis=1).astype(BF16)


def weights_kernel(
    w_one, w_two, w_first, w_last, e_first, e_last, e_force, e_grad,
    m_one, m_two, r_first, r_last, t_force, t_grad,
    stage, taps,
):
    for k, (raw, out) in enumerate(((w_one, m_one), (w_two, m_two))):
        unpack_taps(raw, stage.at[k], taps.at[k])
        fold_middle(taps.at[k], out)
    wf = w_first[...]
    wl = w_last[...]
    pad = jnp.zeros((7, 64), BF16)
    wf = [jnp.concatenate([wf[:, c * 64 : c * 64 + 64], pad], axis=0) for c in range(2)]
    wl = jnp.concatenate([wl, pad], axis=0)
    gap = jnp.zeros((32, 128), BF16)
    for s in range(0, 16, 2):
        cols = slice(s * 64, s * 64 + 128)
        for c in range(2):
            two = [mm(e_first[s + d], wf[c]).astype(BF16) for d in range(2)]
            r_first[c * 128 : c * 128 + 96, cols] = jnp.concatenate(two, axis=1)
            r_first[c * 128 + 96 : c * 128 + 128, cols] = gap
        two = [mm(e_last[s + d], wl).astype(BF16) for d in range(2)]
        r_last[0:96, cols] = jnp.concatenate(two, axis=1)
        r_last[96:128, cols] = gap
    force, grad = [], []
    for p in range(4):
        force.append(mm(e_force[p], wl))
        grad.append(mm(e_grad[p, 0], wf[0]) + mm(e_grad[p, 1], wf[1]))
    t_force[...] = jnp.concatenate(force, axis=1).astype(BF16)
    t_grad[...] = jnp.concatenate(grad, axis=1).astype(BF16)


def fold_weights(w_one, w_two, w_first, w_last, tables):
    big = jax.ShapeDtypeStruct((2304, 256), BF16)
    return pl.pallas_call(
        weights_kernel,
        name="fold_weights",
        out_shape=(
            big, big,
            jax.ShapeDtypeStruct((256, 1024), BF16),
            jax.ShapeDtypeStruct((128, 1024), BF16),
            jax.ShapeDtypeStruct((72, 256), BF16),
            jax.ShapeDtypeStruct((72, 256), BF16),
        ),
        scratch_shapes=[pltpu.VMEM((2, 1024, 128), F32), pltpu.VMEM((2, 25, 64, 64), F32)],
        compiler_params=pltpu.CompilerParams(vmem_limit_bytes=VMEM),
        cost_estimate=pl.CostEstimate(flops=1 << 24, bytes_accessed=1 << 23, transcendentals=0),
    )(w_one, w_two, w_first, w_last, *tables)


def rows_kernel(base, incr, cot, land, storage, source, own, top, bottom):
    wet = land[...].astype(F32)
    images = [base[0], base[1], incr[0], incr[1], cot[...].astype(F32) * wet, wet, storage[...], source[...]]
    rows = land.shape[0]
    for c, image in enumerate(images):
        image = image.astype(F32)
        own[c] = image
        top[c] = image[:HALO]
        bottom[c] = image[rows - HALO :]


def rows_out(*fields):
    rows, cols = fields[3].shape
    edge = jax.ShapeDtypeStruct((8, HALO, cols), F32)
    return pl.pallas_call(
        rows_kernel,
        name="rows_out",
        out_shape=(jax.ShapeDtypeStruct((8, rows, cols), F32), edge, edge),
    )(*fields)


def columns_kernel(own, above, below, turned, nat, west, east):
    rest = jnp.zeros((128 - own.shape[1] - 2 * HALO, 128), F32)
    for c in range(8):
        parts = [above[c], own[c], below[c]]
        if c >= 5:
            nat[c - 5] = jnp.concatenate(parts, axis=0)
        flipped = jnp.concatenate(parts + [rest], axis=0).T
        if c < 6:
            turned[c] = flipped.astype(BF16)
        west[c] = flipped[:HALO]
        east[c] = flipped[128 - HALO :]


def columns_out(own, above, below):
    tall = own.shape[1] + 2 * HALO
    edge = jax.ShapeDtypeStruct((8, HALO, 128), F32)
    return pl.pallas_call(
        columns_kernel,
        name="columns_out",
        out_shape=(
            jax.ShapeDtypeStruct((6, 128, 128), BF16),
            jax.ShapeDtypeStruct((3, tall, 128), F32),
            edge,
            edge,
        ),
    )(own, above, below)


def copy(source, target, sem):
    move = pltpu.make_async_copy(source, target, sem)
    move.start()
    return move


def pipeline(sizes, dot, finish, bufs):
    for k in range(len(sizes) + 1):
        if k < len(sizes):
            dot(k, bufs[k % 2])
        if k:
            finish(k - 1, bufs[(k - 1) % 2])


def pipeline_loop(count, dot, finish, bufs):
    def body(p, _):
        dot(2 * p + 1, bufs[1])
        finish(2 * p, bufs[0])
        dot(2 * p + 2, bufs[0])
        finish(2 * p + 1, bufs[1])
        return 0

    lax.fori_loop(0, (count - 1) // 2, body, 0)
    if count % 2:
        finish(count - 1, bufs[0])
    else:
        dot(count - 1, bufs[1])
        finish(count - 2, bufs[0])
        finish(count - 1, bufs[1])


def three_taps(slots, at, count, weights):
    taps = [slots[pl.ds(at + dc, count)].reshape(count * 80, 768) for dc in range(3)]
    return mm(jnp.concatenate(taps, axis=1), weights[...])


def spread_rows(slot, x0, x1):
    for dr in range(3):
        both = jnp.concatenate([up(x0, dr)[0:40], up(x1, dr)[0:40]], axis=0)
        slot[:, dr * 256 : dr * 256 + 256] = both.astype(BF16)


def thin_taps(table, slots, count, flat_ref, lane):
    for q in range(0, count, 4):
        take = min(4, count - q)
        x = slots[q : q + take].reshape(take * 64, 256)
        flat_ref[:, lane + q * 64 : lane + (q + take) * 64] = mm(table, x, ((1,), (1,)))


def thin_sum(flat_ref, outs):
    span = outs * 64
    total = None
    for dr in range(3):
        part = None
        for dc in range(3):
            tap = flat_ref[(dr * 3 + dc) * 8 : (dr * 3 + dc) * 8 + 8, dc * 64 : dc * 64 + span]
            part = tap if part is None else part + tap
        if dr:
            part = pltpu.roll(part, span - dr, axis=1)
        total = part if total is None else total + part
    return total


def unfold(image, base, pairs, rows, left, right, turn_ref):
    for jp in range(image.shape[1] // 128):
        turn_ref[jp * 8 : jp * 8 + 8, :] = image[:, jp * 128 : jp * 128 + 128]
    picks = []
    for qc in range(2):
        two = [turn_ref[pl.ds(base + qr * 2 + qc, pairs, stride=8), :] for qr in range(2)]
        picks.append(jnp.concatenate(two, axis=1))
    half = exact(left, jnp.concatenate(picks, axis=0), ((1,), (1,)))
    return exact(half[:rows], right[0]) + exact(half[rows:], right[1])


def slab(window, row, k, lhs, lhs_back):
    views = [window[c, pl.ds(row, 16), :] for c in range(6)]

    def stack(c):
        parts = [views[c][:, dr * 128 : dr * 128 + 128] for dr in range(6)]
        parts += [views[5][:, dr * 128 : dr * 128 + 128] for dr in (2, 3)]
        return jnp.concatenate(parts, axis=0).T[:48]

    slabs = [stack(c) for c in range(5)]
    base = jnp.concatenate(slabs[0:2], axis=1)
    incr = jnp.concatenate(slabs[2:4], axis=1)
    lhs[k] = jnp.concatenate([base, incr], axis=0).astype(BF16)
    lhs_back[k] = up(slabs[4], 2).astype(BF16)


def first_products(lhs, lhs_back, seen, r_first, r_last, pre, wet, back_pre, first, count):
    some = slice(first, first + count)
    x = lhs[some].reshape(count * 96, 256)
    y = lhs[some, 0:48, 0:128].reshape(count * 48, 128)
    z = lhs_back[some].reshape(count * 48, 128)
    for jj in range(4):
        lanes = slice(jj * 256, jj * 256 + 256)
        pre[jj, some] = mm(x, r_first[:, lanes]).reshape(count, 96, 256)
        wet[jj, some] = mm(y, seen[:, lanes]).reshape(count, 48, 256)
        back_pre[jj, some] = mm(z, r_last[:, lanes]).reshape(count, 48, 256)


def first_finish(k, jj, pre, wet, slot, keep):
    slope = jnp.tanh(pre[jj, k, 0:48])
    mask = wet[jj, k]
    kept = mask * (1.0 - slope * slope)
    keep[...] = up(kept, 4)[0:40]
    spread_rows(slot, mask * slope, kept * pre[jj, k, 48:96])


def second_finish(pre, mask, slot, keep):
    slope = jnp.tanh(pre[0:40])
    mask = up(mask, 1)[0:40]
    kept = mask * (1.0 - slope * slope)
    keep[...] = up(kept, 2)
    spread_rows(slot, mask * slope, kept * pre[40:80])


def third_finish(pre, mask, back_pre, slot, back):
    rest = jnp.zeros((8, 256), F32)
    slope = jnp.tanh(pre[0:40])
    kept = up(mask, 2)[0:40] * (1.0 - slope * slope)
    slot[0:48] = jnp.concatenate([kept * pre[40:80], rest], axis=0).astype(BF16)
    back[...] = jnp.concatenate([kept * back_pre[0:40], rest], axis=0).astype(BF16)


def inner_kernel(
    turned, pick, seen, m_one_in, m_two_in, r_first, r_last, t_force,
    back_out, two_out, one_out, act_out, flat,
    window, lhs, lhs_back, pre, wet, back_pre, act_one, act_two, tl_three,
    buf_a, buf_b, keep_one, keep_two, back_three, m_one, m_two, sems,
):
    loads = [copy(m_one_in, m_one, sems.at[3]), copy(m_two_in, m_two, sems.at[4])]
    sel = pick[...]
    for c in range(6):
        window[c] = mm(turned[c], sel)
    tl_three[:, 48:64] = jnp.zeros((54, 16, 256), BF16)

    def gather(chunk):
        for k in range(chunk * 5, chunk * 5 + 5):
            slab(window, k * 8, k, lhs, lhs_back)

    def products(chunk):
        first_products(lhs, lhs_back, seen, r_first, r_last, pre, wet, back_pre, chunk * 5, 5)

    def finish_one(chunk):
        for k in range(chunk * 5, chunk * 5 + 5):
            for jj in range(4):
                first_finish(k, jj, pre, wet, act_one.at[k * 4 + jj], keep_one.at[k * 4 + jj])

    gather(0)
    products(0)
    gather(1)
    products(1)
    gather(2)
    finish_one(0)
    products(2)
    finish_one(1)
    loads[0].wait()

    def wet_at(at):
        return wet[at % 4, at // 4]

    def dot_two(q, buf):
        buf[0:640] = three_taps(act_one, q * 8 + 2, 8, m_one)

    def finish_two(q, buf):
        for jj in range(8):
            mask = wet[(jj + 3) % 4, q * 2 + (jj + 3) // 4]
            second_finish(buf[jj * 80 : jj * 80 + 80], mask, act_two.at[q * 8 + jj], keep_two.at[q * 8 + jj])

    dot_two(0, buf_a)
    finish_one(2)
    moves = [copy(keep_one, one_out, sems.at[0])]
    pipeline_loop(7, dot_two, finish_two, (buf_a, buf_b))
    moves.append(copy(keep_two, two_out, sems.at[1]))
    loads[1].wait()
    act_out[0:2] = act_two[0:2]
    act_out[2:4] = act_two[54:56]

    def dot_three(q, buf):
        buf[...] = three_taps(act_two, q * 9, 9, m_two)

    def finish_three(q, buf):
        for jj in range(9):
            at = q * 9 + jj + 4
            third_finish(
                buf[jj * 80 : jj * 80 + 80], wet_at(at), back_pre[at % 4, at // 4],
                tl_three.at[q * 9 + jj], back_three.at[q * 9 + jj],
            )

    dot_three(0, buf_a)
    pipeline_loop(6, dot_three, finish_three, (buf_a, buf_b))
    moves.append(copy(back_three, back_out, sems.at[2]))
    thin_taps(t_force[...], tl_three, 54, flat, 0)
    for move in moves:
        move.wait()


def inner_pass(turned, pick, seen, mats):
    return pl.pallas_call(
        inner_kernel,
        name="inner_pass",
        out_shape=(
            jax.ShapeDtypeStruct((54, 48, 256), BF16),
            jax.ShapeDtypeStruct((56, 40, 256), F32),
            jax.ShapeDtypeStruct((60, 40, 256), F32),
            jax.ShapeDtypeStruct((4, 80, 768), BF16),
            jax.ShapeDtypeStruct((72, 54 * 64), F32),
        ),
        in_specs=[HERE] * 3 + [ANY, ANY] + [HERE] * 3,
        out_specs=(ANY, ANY, ANY, HERE, HERE),
        scratch_shapes=[
            pltpu.VMEM((6, 128, 768), F32),
            pltpu.VMEM((15, 96, 256), BF16),
            pltpu.VMEM((15, 48, 128), BF16),
            pltpu.VMEM((4, 15, 96, 256), F32),
            pltpu.VMEM((4, 15, 48, 256), F32),
            pltpu.VMEM((4, 15, 48, 256), F32),
            pltpu.VMEM((60, 80, 768), BF16),
            pltpu.VMEM((56, 80, 768), BF16),
            pltpu.VMEM((54, 64, 256), BF16),
            pltpu.VMEM((720, 256), F32),
            pltpu.VMEM((720, 256), F32),
            pltpu.VMEM((60, 40, 256), F32),
            pltpu.VMEM((56, 40, 256), F32),
            pltpu.VMEM((54, 48, 256), BF16),
            pltpu.VMEM((2304, 256), BF16),
            pltpu.VMEM((2304, 256), BF16),
            pltpu.SemaphoreType.DMA((5,)),
        ],
        compiler_params=pltpu.CompilerParams(vmem_limit_bytes=VMEM),
        cost_estimate=pl.CostEstimate(flops=1 << 33, bytes_accessed=1 << 23, transcendentals=1 << 21),
    )(turned, pick, seen, *mats)


def outer_kernel(
    far_west, west, east, far_east, nat, pick, seen, m_one_in, m_two_in, r_first, r_last, t_force, left, right,
    act_in, flat_in,
    back_three, keep_two, keep_one, basis, gram,
    window, lhs, lhs_back, pre, wet, back_pre, act_one, act_two, tl_three, buf_a, buf_b, flat, turn, m_one, m_two, sems,
):
    loads = [copy(m_one_in, m_one, sems.at[2]), copy(m_two_in, m_two, sems.at[3])]
    moves = [
        copy(flat_in, flat.at[:, 512 : 512 + 54 * 64], sems.at[0]),
        copy(act_in, act_two.at[8:12], sems.at[1]),
    ]
    sel = pick[...]
    for c in range(6):
        strips = [far_west[c], west[c], east[c], far_east[c]]
        window[c] = mm(jnp.concatenate(strips, axis=0).astype(BF16), sel)
    tl_three[:, 48:64] = jnp.zeros((16, 16, 256), BF16)
    for k in range(6):
        slab(window, (0, 8, 16, 32, 40, 48)[k], k, lhs, lhs_back)
    first_products(lhs, lhs_back, seen, r_first, r_last, pre, wet, back_pre, 0, 6)
    for k in range(6):
        for jj in range(4):
            first_finish(k, jj, pre, wet, act_one.at[k * 4 + jj], keep_one.at[k * 4 + jj])
    loads[0].wait()

    def dot_two(q, buf):
        buf[...] = three_taps(act_one, (2, 14)[q], 8, m_one)

    def finish_two(q, buf):
        for jj in range(8):
            at = (3, 15)[q] + jj
            second_finish(
                buf[jj * 80 : jj * 80 + 80], wet[at % 4, at // 4], act_two.at[(0, 12)[q] + jj], keep_two.at[q * 8 + jj]
            )

    pipeline((8, 8), dot_two, finish_two, (buf_a, buf_b))
    for move in moves + loads[1:]:
        move.wait()

    def dot_three(q, buf):
        buf[...] = three_taps(act_two, (0, 10)[q], 8, m_two)

    def finish_three(q, buf):
        for jj in range(8):
            at = (4, 14)[q] + jj
            third_finish(
                buf[jj * 80 : jj * 80 + 80], wet[at % 4, at // 4], back_pre[at % 4, at // 4],
                tl_three.at[q * 8 + jj], back_three.at[q * 8 + jj],
            )

    pipeline((8, 8), dot_three, finish_three, (buf_a, buf_b))
    thin_taps(t_force[...], tl_three.at[0:8], 8, flat, 0)
    thin_taps(t_force[...], tl_three.at[8:16], 8, flat, 62 * 64)
    turn[...] = jnp.zeros(turn.shape, F32)
    image = thin_sum(flat, 68)
    tall = nat.shape[1]
    force = unfold(image, 0, 40, tall, left[...], right, turn)
    gap = jnp.zeros((128 - 2 * HALO, 128), F32)

    def wide(c):
        rim = jnp.concatenate([far_east[c], gap, far_west[c]], axis=0).T[:tall]
        return jnp.concatenate([nat[c - 5], rim], axis=1)

    mask, storage, source = wide(5), wide(6), wide(7)
    columns = mask.shape[1]
    to_east = mask * pltpu.roll(mask, columns - 1, axis=1)
    to_west = mask * pltpu.roll(mask, 1, axis=1)
    to_north = mask * pltpu.roll(mask, tall - 1, axis=0)
    to_south = mask * pltpu.roll(mask, 1, axis=0)

    def scaled(v):
        total = storage * v + to_east * (v - pltpu.roll(v, columns - 1, axis=1))
        total = total + to_west * (v - pltpu.roll(v, 1, axis=1))
        total = total + to_north * (v - pltpu.roll(v, tall - 1, axis=0))
        total = total + to_south * (v - pltpu.roll(v, 1, axis=0))
        return (total - CENTRE * v) * (1.0 / RADIUS)

    v0 = source + mask * force
    v1 = scaled(v0)
    v2 = 2.0 * scaled(v1) - v0
    v3 = 2.0 * scaled(v2) - v1
    inner = [v[HALO : tall - HALO, 0:128] for v in (v0, v1, v2, v3)]
    for k in range(4):
        basis[k] = inner[k]
    lane = lax.broadcasted_iota(jnp.int32, (8, 128), 1)
    sums = jnp.zeros((8, 128), F32)
    at = 0
    for i in range(4):
        for j in range(i, 4):
            prod = jnp.sum(inner[i] * inner[j], axis=0, keepdims=True)
            value = jnp.sum(prod, axis=1, keepdims=True)
            sums = jnp.where(lane == at, value, sums)
            at += 1
    gram[...] = jnp.broadcast_to(sums, gram.shape)


def outer_pass(strips, nat, pick, seen, mats, left, right, act_in, flat_in, devices):
    tall = nat.shape[1]
    return pl.pallas_call(
        outer_kernel,
        name="outer_pass",
        out_shape=(
            jax.ShapeDtypeStruct((16, 48, 256), BF16),
            jax.ShapeDtypeStruct((16, 40, 256), F32),
            jax.ShapeDtypeStruct((24, 40, 256), F32),
            jax.ShapeDtypeStruct((4, tall - 2 * HALO, 128), F32),
            jax.ShapeDtypeStruct((devices, 8, 128), F32),
        ),
        in_specs=[HERE] * 7 + [ANY, ANY] + [HERE] * 5 + [ANY, ANY],
        scratch_shapes=[
            pltpu.VMEM((6, 64, 768), F32),
            pltpu.VMEM((6, 96, 256), BF16),
            pltpu.VMEM((6, 48, 128), BF16),
            pltpu.VMEM((4, 6, 96, 256), F32),
            pltpu.VMEM((4, 6, 48, 256), F32),
            pltpu.VMEM((4, 6, 48, 256), F32),
            pltpu.VMEM((24, 80, 768), BF16),
            pltpu.VMEM((20, 80, 768), BF16),
            pltpu.VMEM((16, 64, 256), BF16),
            pltpu.VMEM((640, 256), F32),
            pltpu.VMEM((640, 256), F32),
            pltpu.VMEM((72, 70 * 64), F32),
            pltpu.VMEM((320, 128), F32),
            pltpu.VMEM((2304, 256), BF16),
            pltpu.VMEM((2304, 256), BF16),
            pltpu.SemaphoreType.DMA((4,)),
        ],
        compiler_params=pltpu.CompilerParams(vmem_limit_bytes=VMEM),
        cost_estimate=pl.CostEstimate(flops=1 << 32, bytes_accessed=1 << 23, transcendentals=1 << 20),
    )(*strips, nat, pick, seen, *mats, left, right, act_in, flat_in)


def adjoint_kernel(
    back_in, back_rim, two_in, two_rim, one_in, one_rim, m_one_in, m_two_in, t_grad, left, right,
    grad,
    back_three, keep_two, keep_one, three, two, one, buf_a, buf_b, flat, turn, m_one, m_two, m_one_t, m_two_t, sems,
):
    load_two = copy(m_two_in, m_two, sems.at[3, 0])
    def load(inside, rim, target, first, count, pieces, sem):
        moves = [copy(inside, target.at[first : first + count], sem.at[0])]
        for k, (start, stop, to) in enumerate(pieces):
            moves.append(copy(rim.at[start:stop], target.at[to : to + stop - start], sem.at[k + 1]))
        return moves

    moves_three = load(back_in, back_rim, back_three, 8, 54, ((0, 8, 0), (8, 16, 62)), sems.at[0])
    moves_two = load(two_in, two_rim, keep_two, 8, 56, ((0, 8, 0), (8, 16, 64)), sems.at[1])
    moves_one = load(one_in, one_rim, keep_one, 8, 60, ((0, 8, 0), (16, 24, 68)), sems.at[2])
    load_one = copy(m_one_in, m_one, sems.at[3, 1])

    def turn_over(source, target):
        for tap in range(9):
            target[(8 - tap) * 256 : (9 - tap) * 256, :] = source[tap * 256 : tap * 256 + 256, :].T

    load_two.wait()
    turn_over(m_two, m_two_t)
    for move in moves_three:
        move.wait()

    def spread(s, _):
        spread_rows(three.at[s], back_three[s].astype(F32)[0:40], back_three[s + 32].astype(F32)[0:40])
        return 0

    lax.fori_loop(0, 38, spread, 0, unroll=2)
    load_one.wait()
    turn_over(m_one, m_one_t)
    for move in moves_two:
        move.wait()

    def dot_two(q, buf):
        buf[...] = three_taps(three, q * 9, 9, m_two_t)

    def finish_two(q, buf):
        for jj in range(9):
            s = q * 9 + jj
            x0 = buf[jj * 80 : jj * 80 + 40] * keep_two[s + 2]
            x1 = buf[jj * 80 + 40 : jj * 80 + 80] * keep_two[s + 34]
            spread_rows(two.at[s], x0, x1)

    pipeline((9, 9, 9, 9), dot_two, finish_two, (buf_a, buf_b))
    one[:, 48:64] = jnp.zeros((66, 16, 256), BF16)
    rest = jnp.zeros((8, 256), F32)
    for move in moves_one:
        move.wait()
    sizes = (9, 9, 8, 8)

    def dot_one(q, buf):
        buf[0 : sizes[q] * 80] = three_taps(two, sum(sizes[:q]), sizes[q], m_one_t)

    def finish_one(q, buf):
        for jj in range(sizes[q]):
            s = sum(sizes[:q]) + jj
            x0 = buf[jj * 80 : jj * 80 + 40] * keep_one[s + 6]
            x1 = buf[jj * 80 + 40 : jj * 80 + 80] * keep_one[s + 38]
            one[s, 0:48] = jnp.concatenate([x0, rest], axis=0).astype(BF16)
            one[s + 32, 0:48] = jnp.concatenate([x1, rest], axis=0).astype(BF16)

    pipeline(sizes, dot_one, finish_one, (buf_a, buf_b))
    thin_taps(t_grad[...], one, 66, flat, 0)
    image = thin_sum(flat, 64)
    rows = grad.shape[1]
    for ch in range(2):
        grad[ch] = unfold(image, ch * 4, 32, rows, left[...], right, turn)


def adjoint_pass(fields, mats, left, right):
    return pl.pallas_call(
        adjoint_kernel,
        name="adjoint_pass",
        out_shape=jax.ShapeDtypeStruct((2, left.shape[0] // 2, 128), F32),
        in_specs=[ANY] * 8 + [HERE] * 3,
        scratch_shapes=[
            pltpu.VMEM((70, 48, 256), BF16),
            pltpu.VMEM((72, 40, 256), F32),
            pltpu.VMEM((76, 40, 256), F32),
            pltpu.VMEM((38, 80, 768), BF16),
            pltpu.VMEM((36, 80, 768), BF16),
            pltpu.VMEM((66, 64, 256), BF16),
            pltpu.VMEM((720, 256), F32),
            pltpu.VMEM((720, 256), F32),
            pltpu.VMEM((72, 66 * 64), F32),
            pltpu.VMEM((256, 128), F32),
            pltpu.VMEM((2304, 256), BF16),
            pltpu.VMEM((2304, 256), BF16),
            pltpu.VMEM((2304, 256), BF16),
            pltpu.VMEM((2304, 256), BF16),
            pltpu.SemaphoreType.DMA((4, 3)),
        ],
        compiler_params=pltpu.CompilerParams(vmem_limit_bytes=VMEM),
        cost_estimate=pl.CostEstimate(flops=1 << 33, bytes_accessed=1 << 23, transcendentals=0),
    )(*fields, *mats, left, right)


def combine_kernel(basis, gram, surface, residual):
    sums = jnp.sum(gram[...], axis=0)[0:1, :]
    g = {}
    at = 0
    for i in range(4):
        for j in range(i, 4):
            g[i, j] = g[j, i] = sums[:, at : at + 1]
            at += 1

    def inner(a, b):
        total = None
        for i, ai in enumerate(a):
            for j, bj in enumerate(b):
                if ai is not None and bj is not None:
                    term = ai * bj * g[i, j]
                    total = term if total is None else total + term
        return total

    def add(a, b, scale):
        out = []
        for ai, bi in zip(a, b):
            if bi is None:
                out.append(ai)
            else:
                out.append(scale * bi if ai is None else ai + scale * bi)
        return out

    def operate(p):
        out = [None if x is None else CENTRE * x for x in p]
        if p[0] is not None:
            out = add(out, [None, p[0], None, None], RADIUS)
        if p[1] is not None:
            out = add(out, [p[1], None, p[1], None], 0.5 * RADIUS)
        if p[2] is not None:
            out = add(out, [None, p[2], None, p[2]], 0.5 * RADIUS)
        return out

    unit = jnp.ones((1, 1), F32)
    r = [unit, None, None, None]
    p = [unit, None, None, None]
    x = [None] * 4
    norm = g[0, 0]
    for step in range(3):
        image = operate(p)
        alpha = norm / inner(p, image)
        x = add(x, p, alpha)
        r = add(r, image, -alpha)
        if step < 2:
            new = inner(r, r)
            p = add(r, p, new / norm)
            norm = new
    surface[...] = x[0] * basis[0] + x[1] * basis[1] + x[2] * basis[2]
    residual[...] = r[0] * basis[0] + r[1] * basis[1] + r[2] * basis[2] + r[3] * basis[3]


def combine(basis, gram):
    shape = jax.ShapeDtypeStruct(basis.shape[1:], F32)
    return pl.pallas_call(combine_kernel, name="combine", out_shape=(shape, shape))(basis, gram)


def shards(
    base_state,
    increment,
    cotangent,
    land_sea,
    storage,
    source,
    w_first,
    w_middle_one,
    w_middle_two,
    w_last,
):
    rows = land_sea.shape[0]
    tall = rows + 2 * HALO
    gx, gy = lax.axis_size("gx"), lax.axis_size("gy")
    own, top, bottom = rows_out(base_state, increment, cotangent, land_sea, storage, source)
    above = lax.ppermute(bottom, "gy", [(i, i + 1) for i in range(gy - 1)])
    below = lax.ppermute(top, "gy", [(i + 1, i) for i in range(gy - 1)])

    e_first, e_last, e_force, e_grad, seen = one_hots()
    m_one, m_two, r_first, r_last, t_force, t_grad = fold_weights(
        w_middle_one, w_middle_two, w_first, w_last, (e_first, e_last, e_force, e_grad)
    )
    turned, nat, west, east = columns_out(own, above, below)
    far_west = lax.ppermute(east, "gx", [(i, (i + 1) % gx) for i in range(gx)])
    far_east = lax.ppermute(west, "gx", [((i + 1) % gx, i) for i in range(gx)])
    pick = decimate()
    mats = (m_one, m_two, r_first, r_last, t_force)
    back_in, two_in, one_in, act_in, flat_in = inner_pass(turned, pick, seen, mats)
    left, right = unfold_tables(tall, 36, 12, 40, 256, -4)
    back_rim, two_rim, one_rim, basis, gram = outer_pass(
        (far_west, west, east, far_east), nat, pick, seen, mats, left, right, act_in, flat_in, gx * gy
    )
    gram = lax.all_to_all(gram, ("gx", "gy"), 0, 0)
    left, right = unfold_tables(rows, 32, 0, 32, 128, 0)
    fields = (back_in, back_rim, two_in, two_rim, one_in, one_rim)
    grad = adjoint_pass(fields, (m_one, m_two, t_grad), left, right)
    surface, residual = combine(basis, gram)
    return (grad, surface, residual)


def solution(mesh):
    placed = (
        P(None, "gy", "gx"),
        P(None, "gy", "gx"),
        P("gy", "gx"),
        P("gy", "gx"),
        P("gy", "gx"),
        P("gy", "gx"),
        P(),
        P(),
        P(),
        P(),
    )
    return jax.shard_map(
        shards,
        mesh=mesh,
        in_specs=placed,
        out_specs=(P(None, "gy", "gx"), P("gy", "gx"), P("gy", "gx")),
        check_vma=False,
    )
```

time: 103 us -> 71.9 us (0.70)
  waiting for transfers between devices: 20.2 us -> 0.33 us
  other arithmetic: 5.24 us -> 0 us
  Pallas kernels: 58.5 us -> 53.7 us
  local copies, waits for them, and re-layouts: 4.12 us -> 1.91 us
  starting transfers between devices: 13.7 us -> 14.8 us
    ppermute x9 -> x4, waiting for transfers between devices: 20.2 us -> 0.33 us  [the longest x1 0.32 us: shards(): below = lax.ppermute(top, 'gy', [(i + 1, i) for i in range(gy - 1)])]
    all_to_all x0 -> x1, starting transfers between devices: none -> 6.08 us  [shards(): gram = lax.all_to_all(gram, ('gx', 'gy'), 0, 0)]
    ppermute x9 -> x4, starting transfers between devices: 13.7 us -> 8.72 us  [the longest x1 3.03 us: shards(): far_east = lax.ppermute(west, 'gx', [((i + 1) % gx, i) for i in range(gx)])]
    unnamed x4 -> x0, other arithmetic: 3.01 us -> none
    reshape x2 -> x0, local copies, waits for them, and re-layouts: 2.33 us -> none  [the longest x1 1.17 us: shards(): w_middle_one.reshape(25, 64, 64)]
    pallas_call x1, Pallas kernels: 16.9 us -> 14.8 us  [adjoint_pass(): pl.pallas_call(adjoint_kernel, name='adjoint_pass', out_shape=jax.ShapeDt...]
    pallas_call x1 -> x4, Pallas kernels: 35.1 us -> 33.2 us  [the longest x1 20.8 us: inner_pass(): pl.pallas_call(inner_kernel, name='inner_pass', out_shape=(jax.ShapeDtype...]
    add x5 -> x0, other arithmetic: 1.3 us -> none  [everywhere(): x = x + lax.ppermute(x, axis, [(i, i ^ step) for i in range(count)])]
  transfers between devices with their start and end apart: 9 -> 5, of which waited for: 6 -> 1; matrix products, arithmetic and copies ran while one was open for 2% -> 0% of each run, Pallas kernels for 21% -> 55%
where the time goes in v2:
time: 71.9 us; the launch traced here: 71.5 us
  Pallas kernels  53.7 us (75%)
  starting transfers between devices  14.8 us (21%)
  local copies, waits for them, and re-layouts  1.91 us (3%)
  between operations  0.74 us (1%)
    pallas_call x1, Pallas kernels, inner_pass(): pl.pallas_call(inner_kernel, name='inner_pass', out_shape=(jax.ShapeDtype...  20.8 us
    pallas_call x1, Pallas kernels, adjoint_pass(): pl.pallas_call(adjoint_kernel, name='adjoint_pass', out_shape=jax.ShapeDt...  14.8 us
    pallas_call x1, Pallas kernels, outer_pass(): pl.pallas_call(outer_kernel, name='outer_pass', out_shape=(jax.ShapeDtype...  8.88 us
    all_to_all x1, starting transfers between devices, shards(): gram = lax.all_to_all(gram, ('gx', 'gy'), 0, 0)  6.08 us
    pallas_call x1, Pallas kernels, fold_weights(): pl.pallas_call(weights_kernel, name='fold_weights', out_shape=(big, big,...  3.83 us
    ppermute x1, starting transfers between devices, shards(): far_east = lax.ppermute(west, 'gx', [((i + 1) % gx, i) for i in range(gx)])  3.03 us
    ppermute x1, starting transfers between devices, shards(): above = lax.ppermute(bottom, 'gy', [(i, i + 1) for i in range(gy - 1)])  2.35 us
    ppermute x1, starting transfers between devices, shards(): far_west = lax.ppermute(east, 'gx', [(i, (i + 1) % gx) for i in range(gx)])  2.05 us
  transfers between devices with their start and end apart: 5, of which 1 were waited for; matrix products, arithmetic and copies ran while one was open for 0% of the time, Pallas kernels for 55%

profile of v2, /device:TPU:0, one launch (start us, length us, event | category | flops | bytes accessed | tf_op | source)
XLA Modules:
  0.0 71.5 jit_solution(8464617523485034782)
XLA Ops:
  0.6 1.6 %rows_out.1 = (f32[8,64,128]{2,1,0:T(8,128)}, f32[8,16,128]{2,1,0:T(8,128)}, f32[8,16,128]{2,1,0:T(8,128)}) custom-call(bf16[2,64,128]{2,1,0:T(8,128)(2,1)} %base.1, bf16[2,64,128]{2,1,0:T(8,128)(2,1)} %incr.1, bf16[64,128]{1,0:T(8,128)(2,1)} %cot.1, s32[64,128]{1,0:T(8,128)} %land.1, f32[64,128]{1,0:T(8,128)} %storage.1, f32[64,128]{1,0:T(8,128)} %source.1), custom_call_target="tpu_custom_call" | custom-call | tf_op jit(solution)/shard_map/rows_out/pallas_call | solution.py:178
  2.2 2.3 %collective-permute-start = (f32[8,16,128]{2,1,0:T(8,128)}, f32[8,16,128]{2,1,0:T(8,128)S(1)}, u32[]{:S(2)}, u32[]{:S(2)}) collective-permute-start(f32[8,16,128]{2,1,0:T(8,128)} %get-tuple-element.29), channel_id=1, source_target_pairs={{0,1},{1,2},{2,3},{4,5},{5,6},{6,7},{8,9},{9,10},{10,11},{12,13},{... | collective-permute-start | bytes 196616 | tf_op jit(solution)/shard_map/ppermute | solution.py:755
  4.6 1.3 %collective-permute-start.1 = (f32[8,16,128]{2,1,0:T(8,128)}, f32[8,16,128]{2,1,0:T(8,128)S(1)}, u32[]{:S(2)}, u32[]{:S(2)}) collective-permute-start(f32[8,16,128]{2,1,0:T(8,128)} %get-tuple-element.30), channel_id=1, source_target_pairs={{1,0},{2,1},{3,2},{5,4},{6,5},{7,6},{9,8},{10,9},{11,10},{13,12},{... | collective-permute-start | bytes 196616 | tf_op jit(solution)/shard_map/ppermute | solution.py:756
  5.9 3.8 %fold_weights.1 = (bf16[2304,256]{1,0:T(8,128)(2,1)}, bf16[2304,256]{1,0:T(8,128)(2,1)}, bf16[256,1024]{1,0:T(8,128)(2,1)}, bf16[128,1024]{1,0:T(8,128)(2,1)}, b...) custom-call(bf16[25,4096]{1,0:T(8,128)(2,1)} %w_one.1, bf16[25,4096]{1,0:T(8,128)(2,1)} %w_two.1, ...), custom_call_target="tpu_custom_call" | custom-call | flops 16777216 | bytes 8388608 | tf_op jit(solution)/shard_map/fold_weights/pallas_call | solution.py:148
  9.7 0.0 collective-permute-done.above
  9.7 0.0 copy-start.1
  9.7 0.3 collective-permute-done.1.below
  10.0 0.0 copy-start.2
  10.0 0.3 copy-done.1
  10.3 0.3 copy-done.2
  10.7 1.9 %columns_out.1 = (bf16[6,128,128]{2,1,0:T(8,128)(2,1)}, f32[3,96,128]{2,1,0:T(8,128)}, f32[8,16,128]{2,1,0:T(8,128)}, f32[8,16,128]{2,1,0:T(8,128)}) custom-call(f32[8,64,128]{2,1,0:T(8,128)} %get-tuple-element.28.own, f32[8,16,128]{2,1,0:T(8,128)} %copy-done.1, f32[8,16,128]{2,1,0:T(8,128)} %copy-done.2), custom_call_target="tpu_custom_call" | custom-call | tf_op jit(solution)/shard_map/columns_out/pallas_call | solution.py:201
  12.6 2.0 %collective-permute-start.2 = (f32[8,16,128]{2,1,0:T(8,128)}, f32[8,16,128]{2,1,0:T(8,128)S(1)}, u32[]{:S(2)}, u32[]{:S(2)}) collective-permute-start(f32[8,16,128]{2,1,0:T(8,128)} %get-tuple-element.38.east), channel_id=1, source_target_pairs={{0,4},{4,8},{8,12},{12,16},{16,20},{20,24},{24,28},{28,0},{1,5},{5... | collective-permute-start | bytes 196616 | tf_op jit(solution)/shard_map/ppermute | solution.py:763
  14.6 3.0 %collective-permute-start.3 = (f32[8,16,128]{2,1,0:T(8,128)}, f32[8,16,128]{2,1,0:T(8,128)S(1)}, u32[]{:S(2)}, u32[]{:S(2)}) collective-permute-start(f32[8,16,128]{2,1,0:T(8,128)} %get-tuple-element.39.west), channel_id=1, source_target_pairs={{4,0},{8,4},{12,8},{16,12},{20,16},{24,20},{28,24},{0,28},{5,1},{9... | collective-permute-start | bytes 196616 | tf_op jit(solution)/shard_map/ppermute | solution.py:764
  17.7 20.8 %inner_pass.1 = (bf16[54,48,256]{2,1,0:T(8,128)(2,1)}, f32[56,40,256]{2,1,0:T(8,128)}, f32[60,40,256]{2,1,0:T(8,128)}, bf16[4,80,768]{2,1,0:T(8,128)(2,1)}, f32[72,3456]{1,0:T(8,128)}) custom-call(bf16[6,128,128]{2,1,0:T(8,128)(2,1)} %get-tuple-element.31.turned, bf16[128,768]{1,0:T(8,128)(2,1)} %constant.25.clone.pick, ...), custom_call_target="tpu_custom_call" | custom-call | flops 8589934592 | bytes 8388608 | tf_op jit(solution)/shard_map/inner_pass/pallas_call | solution.py:412
  38.5 0.0 collective-permute-done.2.far_west
  38.5 0.0 copy-start.3
  38.6 0.0 collective-permute-done.3.far_east
  38.6 0.0 copy-start.4
  38.6 0.6 copy-done.3
  39.2 0.0 copy-done.4
  39.2 8.9 %outer_pass.1 = (bf16[16,48,256]{2,1,0:T(8,128)(2,1)}, f32[16,40,256]{2,1,0:T(8,128)}, f32[24,40,256]{2,1,0:T(8,128)}, f32[4,64,128]{2,1,0:T(8,128)}, f32[32,8,128]{2,1,0:T(8,128)}) custom-call(f32[8,16,128]{2,1,0:T(8,128)} %copy-done.3, f32[8,16,128]{2,1,0:T(8,128)} %get-tuple-element.39.west, f32[8,16,128]{2,1,0:T(8,128)} %get-tuple-element.38.east, ...), custom_call_target="tpu_custom_call" | custom-call | flops 4294967296 | bytes 8388608 | tf_op jit(solution)/shard_map/outer_pass/pallas_call | solution.py:545
  48.1 6.1 %all-to-all-start = ((f32[32,8,128]{2,1,0:T(8,128)}), f32[32,8,128]{2,1,0:T(8,128)S(1)}, u32[]{:S(2)}, u32[]{:S(2)}) async-start(f32[32,8,128]{2,1,0:T(8,128)} %get-tuple-element.50), calls=%async_computation | async-start | bytes 262144 | tf_op jit(solution)/shard_map/all_to_all | solution.py:772
  54.2 14.8 %adjoint_pass.1 = f32[2,64,128]{2,1,0:T(8,128)} custom-call(bf16[54,48,256]{2,1,0:T(8,128)(2,1)} %get-tuple-element.37.back_in, bf16[16,48,256]{2,1,0:T(8,128)(2,1)} %get-tuple-element.43.back_rim, f32[56,40,256]{2,1,0:T(8,128)} %get-tuple-element.44.two_in, f32[16,40,256]{2,1,0:T(8,128)} %get-tuple-element.45.two_rim, ...), custom_call_target="tpu_custom_call" | custom-call | flops 8589934592 | bytes 8388608 | tf_op jit(solution)/shard_map/adjoint_pass/pallas_call | solution.py:652
  69.0 0.0 all-to-all-done.gram
  69.0 0.0 copy-start
  69.0 0.6 copy-done
  69.7 1.8 %combine.1 = (f32[64,128]{1,0:T(8,128)}, f32[64,128]{1,0:T(8,128)}) custom-call(f32[4,64,128]{2,1,0:T(8,128)} %get-tuple-element.49.basis, f32[32,8,128]{2,1,0:T(8,128)} %copy-done), custom_call_target="tpu_custom_call" | custom-call | tf_op jit(solution)/shard_map/combine/pallas_call | solution.py:736
Async XLA Ops:
  2.2 7.5 %collective-permute-start = (f32[8,16,128]{2,1,0:T(8,128)}, f32[8,16,128]{2,1,0:T(8,128)S(1)}, u32[]{:S(2)}, u32[]{:S(2)}) collective-permute-start(f32[8,16,128]{2,1,0:T(8,128)} %get-tuple-element.29), channel_id=1, source_target_pairs={{0,1},{1,2},{2,3},{4,5},{5,6},{6,7},{8,9},{9,10},{10,11},{12,13},{... | collective-permute-start | bytes 196616 | tf_op jit(solution)/shard_map/ppermute | solution.py:755
  4.6 5.5 %collective-permute-start.1 = (f32[8,16,128]{2,1,0:T(8,128)}, f32[8,16,128]{2,1,0:T(8,128)S(1)}, u32[]{:S(2)}, u32[]{:S(2)}) collective-permute-start(f32[8,16,128]{2,1,0:T(8,128)} %get-tuple-element.30), channel_id=1, source_target_pairs={{1,0},{2,1},{3,2},{5,4},{6,5},{7,6},{9,8},{10,9},{11,10},{13,12},{... | collective-permute-start | bytes 196616 | tf_op jit(solution)/shard_map/ppermute | solution.py:756
  9.7 0.6 copy-start.1
  10.0 0.6 copy-start.2
  12.6 25.9 %collective-permute-start.2 = (f32[8,16,128]{2,1,0:T(8,128)}, f32[8,16,128]{2,1,0:T(8,128)S(1)}, u32[]{:S(2)}, u32[]{:S(2)}) collective-permute-start(f32[8,16,128]{2,1,0:T(8,128)} %get-tuple-element.38.east), channel_id=1, source_target_pairs={{0,4},{4,8},{8,12},{12,16},{16,20},{20,24},{24,28},{28,0},{1,5},{5... | collective-permute-start | bytes 196616 | tf_op jit(solution)/shard_map/ppermute | solution.py:763
  14.6 23.9 %collective-permute-start.3 = (f32[8,16,128]{2,1,0:T(8,128)}, f32[8,16,128]{2,1,0:T(8,128)S(1)}, u32[]{:S(2)}, u32[]{:S(2)}) collective-permute-start(f32[8,16,128]{2,1,0:T(8,128)} %get-tuple-element.39.west), channel_id=1, source_target_pairs={{4,0},{8,4},{12,8},{16,12},{20,16},{24,20},{28,24},{0,28},{5,1},{9... | collective-permute-start | bytes 196616 | tf_op jit(solution)/shard_map/ppermute | solution.py:764
  38.5 0.6 copy-start.3
  38.6 0.6 copy-start.4
  48.1 20.9 %all-to-all-start = ((f32[32,8,128]{2,1,0:T(8,128)}), f32[32,8,128]{2,1,0:T(8,128)S(1)}, u32[]{:S(2)}, u32[]{:S(2)}) async-start(f32[32,8,128]{2,1,0:T(8,128)} %get-tuple-element.50), calls=%async_computation | async-start | bytes 262144 | tf_op jit(solution)/shard_map/all_to_all | solution.py:772
  69.0 0.7 copy-start

commit v3 on v2

--- a/solution.py
+++ b/solution.py
@@ -13,7 +13,7 @@
 HALO = 16
 CENTRE = 6.125
 RADIUS = 5.875
-VMEM = 60 * 1024 * 1024
+MIB = 1024 * 1024
 ANY = pl.BlockSpec(memory_space=pl.ANY)
 HERE = pl.BlockSpec(memory_space=pltpu.VMEM)
 
@@ -59,7 +59,7 @@
 
 def unfold_tables(rows, blocks, first_row, pairs, width, first_col):
     left = np.zeros((2 * rows, 256), np.float32)
-    right = np.zeros((2, 2 * pairs, width), np.float32)
+    right = np.zeros((4 * pairs, width), np.float32)
     for par in range(2):
         for qr in range(2):
             for i in range(blocks):
@@ -70,7 +70,7 @@
             for jp in range(pairs):
                 col = 4 * jp + 2 * par + qc + first_col
                 if -HALO <= col < 128 + HALO:
-                    right[par, qc * pairs + jp, col % width] = 1
+                    right[(par * 2 + qc) * pairs + jp, col % width] = 1
     return jnp.asarray(left), jnp.asarray(right)
 
 
@@ -156,9 +156,15 @@
             jax.ShapeDtypeStruct((72, 256), BF16),
         ),
         scratch_shapes=[pltpu.VMEM((2, 1024, 128), F32), pltpu.VMEM((2, 25, 64, 64), F32)],
-        compiler_params=pltpu.CompilerParams(vmem_limit_bytes=VMEM),
+        compiler_params=pltpu.CompilerParams(vmem_limit_bytes=60 * MIB),
         cost_estimate=pl.CostEstimate(flops=1 << 24, bytes_accessed=1 << 23, transcendentals=0),
     )(w_one, w_two, w_first, w_last, *tables)
+
+
+def copy(source, target, sem):
+    move = pltpu.make_async_copy(source, target, sem)
+    move.start()
+    return move
 
 
 def rows_kernel(base, incr, cot, land, storage, source, own, top, bottom):
@@ -182,63 +188,27 @@
     )(*fields)
 
 
-def columns_kernel(own, above, below, turned, nat, west, east):
+def columns_kernel(own, above, below, images, west, east):
     rest = jnp.zeros((128 - own.shape[1] - 2 * HALO, 128), F32)
     for c in range(8):
-        parts = [above[c], own[c], below[c]]
+        image = jnp.concatenate([above[c], own[c], below[c], rest], axis=0)
+        flipped = image.T
+        if c < 6:
+            images[c] = flipped
         if c >= 5:
-            nat[c - 5] = jnp.concatenate(parts, axis=0)
-        flipped = jnp.concatenate(parts + [rest], axis=0).T
-        if c < 6:
-            turned[c] = flipped.astype(BF16)
+            images[c + 1] = image
         west[c] = flipped[:HALO]
         east[c] = flipped[128 - HALO :]
 
 
 def columns_out(own, above, below):
-    tall = own.shape[1] + 2 * HALO
     edge = jax.ShapeDtypeStruct((8, HALO, 128), F32)
     return pl.pallas_call(
         columns_kernel,
         name="columns_out",
-        out_shape=(
-            jax.ShapeDtypeStruct((6, 128, 128), BF16),
-            jax.ShapeDtypeStruct((3, tall, 128), F32),
-            edge,
-            edge,
-        ),
+        out_shape=(jax.ShapeDtypeStruct((9, 128, 128), F32), edge, edge),
+        compiler_params=pltpu.CompilerParams(vmem_limit_bytes=4 * MIB),
     )(own, above, below)
-
-
-def copy(source, target, sem):
-    move = pltpu.make_async_copy(source, target, sem)
-    move.start()
-    return move
-
-
-def pipeline(sizes, dot, finish, bufs):
-    for k in range(len(sizes) + 1):
-        if k < len(sizes):
-            dot(k, bufs[k % 2])
-        if k:
-            finish(k - 1, bufs[(k - 1) % 2])
-
-
-def pipeline_loop(count, dot, finish, bufs):
-    def body(p, _):
-        dot(2 * p + 1, bufs[1])
-        finish(2 * p, bufs[0])
-        dot(2 * p + 2, bufs[0])
-        finish(2 * p + 1, bufs[1])
-        return 0
-
-    lax.fori_loop(0, (count - 1) // 2, body, 0)
-    if count % 2:
-        finish(count - 1, bufs[0])
-    else:
-        dot(count - 1, bufs[1])
-        finish(count - 2, bufs[0])
-        finish(count - 1, bufs[1])
 
 
 def three_taps(slots, at, count, weights):
@@ -273,15 +243,21 @@
     return total
 
 
-def unfold(image, base, pairs, rows, left, right, turn_ref):
+def unfold(image, fields, pairs, left, right, turn_ref):
     for jp in range(image.shape[1] // 128):
         turn_ref[jp * 8 : jp * 8 + 8, :] = image[:, jp * 128 : jp * 128 + 128]
     picks = []
-    for qc in range(2):
-        two = [turn_ref[pl.ds(base + qr * 2 + qc, pairs, stride=8), :] for qr in range(2)]
-        picks.append(jnp.concatenate(two, axis=1))
+    for f in range(fields):
+        for qc in range(2):
+            two = [turn_ref[pl.ds(f * 4 + qr * 2 + qc, pairs, stride=8), :] for qr in range(2)]
+            picks.append(jnp.concatenate(two, axis=1))
     half = exact(left, jnp.concatenate(picks, axis=0), ((1,), (1,)))
-    return exact(half[:rows], right[0]) + exact(half[rows:], right[1])
+    rows, span = half.shape[0] // 2, 2 * pairs
+    parts = []
+    for f in range(fields):
+        two = [half[par * rows : par * rows + rows, f * span : f * span + span] for par in range(2)]
+        parts.append(jnp.concatenate(two, axis=1))
+    return exact(jnp.concatenate(parts, axis=0), right)
 
 
 def slab(window, row, k, lhs, lhs_back):
@@ -332,20 +308,34 @@
     slope = jnp.tanh(pre[0:40])
     kept = up(mask, 2)[0:40] * (1.0 - slope * slope)
     slot[0:48] = jnp.concatenate([kept * pre[40:80], rest], axis=0).astype(BF16)
-    back[...] = jnp.concatenate([kept * back_pre[0:40], rest], axis=0).astype(BF16)
+    back[...] = kept * back_pre[0:40]
+
+
+def turn_over(source, target, tap):
+    target[(8 - tap) * 256 : (9 - tap) * 256, :] = source[tap * 256 : tap * 256 + 256, :].T
 
 
 def inner_kernel(
-    turned, pick, seen, m_one_in, m_two_in, r_first, r_last, t_force,
-    back_out, two_out, one_out, act_out, flat,
+    images, pick, seen_in, m_one_in, m_two_in, r_first_in, r_last_in, t_force, t_grad,
+    back_out, two_out, one_out, act_out, m_one_out, m_two_out, force_out, grad_out,
     window, lhs, lhs_back, pre, wet, back_pre, act_one, act_two, tl_three,
-    buf_a, buf_b, keep_one, keep_two, back_three, m_one, m_two, sems,
+    buf_a, buf_b, keep_one, keep_two, back_three, m_one, m_two, m_one_t, m_two_t, one, flat,
+    seen, r_first, r_last, sems,
 ):
-    loads = [copy(m_one_in, m_one, sems.at[3]), copy(m_two_in, m_two, sems.at[4])]
+    tables = [
+        copy(r_first_in, r_first, sems.at[2]),
+        copy(seen_in, seen, sems.at[3]),
+        copy(r_last_in, r_last, sems.at[4]),
+    ]
+    loads = [copy(m_one_in, m_one, sems.at[0]), copy(m_two_in, m_two, sems.at[1])]
     sel = pick[...]
     for c in range(6):
-        window[c] = mm(turned[c], sel)
+        window[c] = mm(images[c].astype(BF16), sel)
     tl_three[:, 48:64] = jnp.zeros((54, 16, 256), BF16)
+    one[:, 48:64] = jnp.zeros((50, 16, 256), BF16)
+    force_out[...] = jnp.zeros(force_out.shape, F32)
+    grad_out[...] = jnp.zeros(grad_out.shape, F32)
+    flat[:, 0:128] = jnp.zeros((72, 128), F32)
 
     def gather(chunk):
         for k in range(chunk * 5, chunk * 5 + 5):
@@ -360,6 +350,8 @@
                 first_finish(k, jj, pre, wet, act_one.at[k * 4 + jj], keep_one.at[k * 4 + jj])
 
     gather(0)
+    for table in tables:
+        table.wait()
     products(0)
     gather(1)
     products(1)
@@ -367,7 +359,8 @@
     finish_one(0)
     products(2)
     finish_one(1)
-    loads[0].wait()
+    for load in loads:
+        load.wait()
 
     def wet_at(at):
         return wet[at % 4, at // 4]
@@ -377,50 +370,120 @@
 
     def finish_two(q, buf):
         for jj in range(8):
-            mask = wet[(jj + 3) % 4, q * 2 + (jj + 3) // 4]
-            second_finish(buf[jj * 80 : jj * 80 + 80], mask, act_two.at[q * 8 + jj], keep_two.at[q * 8 + jj])
-
+            k = q * 8 + jj
+            second_finish(buf[jj * 80 : jj * 80 + 80], wet_at(k + 3), act_two.at[k], keep_two.at[k])
+        for tap in range(q * 2, min(q * 2 + 2, 9)):
+            turn_over(m_two, m_two_t, tap)
+
+    def dot_three(q, buf):
+        buf[...] = three_taps(act_two, q * 9, 9, m_two)
+
+    def finish_three(q, buf):
+        for jj in range(9):
+            k = q * 9 + jj
+            at = k + 4
+            third_finish(
+                buf[jj * 80 : jj * 80 + 80], wet_at(at), back_pre[at % 4, at // 4], tl_three.at[k], back_three.at[k]
+            )
+        for tap in range(q * 2, min(q * 2 + 2, 9)):
+            turn_over(m_one, m_one_t, tap)
+        first, last = q * 9 // 4 * 4, (q * 9 + 9) // 4 * 4 if q < 5 else 54
+        thin_taps(t_force[...], tl_three.at[first:last], last - first, flat, 128 + first * 64)
+
+    bufs = (buf_a, buf_b)
     dot_two(0, buf_a)
     finish_one(2)
-    moves = [copy(keep_one, one_out, sems.at[0])]
-    pipeline_loop(7, dot_two, finish_two, (buf_a, buf_b))
-    moves.append(copy(keep_two, two_out, sems.at[1]))
-    loads[1].wait()
+    for q in range(1, 7):
+        dot_two(q, bufs[q % 2])
+        finish_two(q - 1, bufs[(q - 1) % 2])
+    finish_two(6, buf_a)
+    moves = [
+        copy(m_two_t, m_two_out, sems.at[0]),
+        copy(keep_one.at[4:6], one_out, sems.at[1]),
+        copy(keep_two.at[0:4], two_out.at[0:4], sems.at[2]),
+        copy(keep_two.at[52:56], two_out.at[4:8], sems.at[3]),
+    ]
     act_out[0:2] = act_two[0:2]
     act_out[2:4] = act_two[54:56]
-
-    def dot_three(q, buf):
-        buf[...] = three_taps(act_two, q * 9, 9, m_two)
-
-    def finish_three(q, buf):
+    dot_three(0, buf_a)
+    for q in range(1, 6):
+        dot_three(q, bufs[q % 2])
+        finish_three(q - 1, bufs[(q - 1) % 2])
+    finish_three(5, buf_b)
+    moves += [
+        copy(m_one_t, m_one_out, sems.at[4]),
+        copy(back_three.at[0:4], back_out.at[0:4], sems.at[5]),
+        copy(back_three.at[50:54], back_out.at[4:8], sems.at[6]),
+    ]
+
+    three, two = act_one, act_two
+    for s in range(29):
+        spread_rows(three.at[s], back_three[s], back_three[s + 25])
+
+    def dot_back_two(q, buf):
+        buf[...] = three_taps(three, q * 9, 9, m_two_t)
+
+    def finish_back_two(q, buf):
         for jj in range(9):
-            at = q * 9 + jj + 4
-            third_finish(
-                buf[jj * 80 : jj * 80 + 80], wet_at(at), back_pre[at % 4, at // 4],
-                tl_three.at[q * 9 + jj], back_three.at[q * 9 + jj],
-            )
-
-    dot_three(0, buf_a)
-    pipeline_loop(6, dot_three, finish_three, (buf_a, buf_b))
-    moves.append(copy(back_three, back_out, sems.at[2]))
-    thin_taps(t_force[...], tl_three, 54, flat, 0)
+            s = q * 9 + jj
+            x0 = buf[jj * 80 : jj * 80 + 40] * keep_two[s + 2]
+            x1 = buf[jj * 80 + 40 : jj * 80 + 80] * keep_two[s + 27]
+            spread_rows(two.at[s], x0, x1)
+
+    starts, rest = (0, 8, 16, 25), jnp.zeros((8, 256), F32)
+    groups = (((0, 8), (26, 32)), ((8, 16), (32, 40)), ((16, 26), (40, 50)))
+
+    def dot_back_one(q, buf):
+        count = starts[q + 1] - starts[q]
+        buf[0 : count * 80] = three_taps(two, starts[q], count, m_one_t)
+
+    def finish_back_one(q, buf):
+        for jj in range(starts[q + 1] - starts[q]):
+            s = starts[q] + jj
+            x0 = buf[jj * 80 : jj * 80 + 40] * keep_one[s + 6]
+            x1 = buf[jj * 80 + 40 : jj * 80 + 80] * keep_one[s + 31]
+            one[s, 0:48] = jnp.concatenate([x0, rest], axis=0).astype(BF16)
+            one[s + 25, 0:48] = jnp.concatenate([x1, rest], axis=0).astype(BF16)
+        for first, last in groups[q]:
+            thin_taps(t_grad[...], one.at[first:last], last - first, flat, 128 + first * 64)
+
+    dot_back_two(0, buf_a)
+    flat[:, 128 + 54 * 64 :] = jnp.zeros((72, 128), F32)
+    force_out[:, 384 : 384 + 56 * 64] = thin_sum(flat, 56)
+    dot_back_two(1, buf_b)
+    finish_back_two(0, buf_a)
+    dot_back_two(2, buf_a)
+    finish_back_two(1, buf_b)
+    finish_back_two(2, buf_a)
+    flat[:, 128 + 50 * 64 : 256 + 50 * 64] = jnp.zeros((72, 128), F32)
+    dot_back_one(0, buf_a)
+    dot_back_one(1, buf_b)
+    finish_back_one(0, buf_a)
+    dot_back_one(2, buf_a)
+    finish_back_one(1, buf_b)
+    finish_back_one(2, buf_a)
+    grad_out[:, 384 : 384 + 52 * 64] = thin_sum(flat, 52)
     for move in moves:
         move.wait()
 
 
-def inner_pass(turned, pick, seen, mats):
+def inner_pass(images, pick, seen, mats, t_grad):
+    big = jax.ShapeDtypeStruct((2304, 256), BF16)
     return pl.pallas_call(
         inner_kernel,
         name="inner_pass",
         out_shape=(
-            jax.ShapeDtypeStruct((54, 48, 256), BF16),
-            jax.ShapeDtypeStruct((56, 40, 256), F32),
-            jax.ShapeDtypeStruct((60, 40, 256), F32),
+            jax.ShapeDtypeStruct((8, 40, 256), F32),
+            jax.ShapeDtypeStruct((8, 40, 256), F32),
+            jax.ShapeDtypeStruct((2, 40, 256), F32),
             jax.ShapeDtypeStruct((4, 80, 768), BF16),
-            jax.ShapeDtypeStruct((72, 54 * 64), F32),
+            big,
+            big,
+            jax.ShapeDtypeStruct((8, 68 * 64), F32),
+            jax.ShapeDtypeStruct((8, 64 * 64), F32),
         ),
-        in_specs=[HERE] * 3 + [ANY, ANY] + [HERE] * 3,
-        out_specs=(ANY, ANY, ANY, HERE, HERE),
+        in_specs=[HERE] * 2 + [ANY] * 5 + [HERE] * 2,
+        out_specs=(ANY, ANY, ANY, HERE, ANY, ANY, HERE, HERE),
         scratch_shapes=[
             pltpu.VMEM((6, 128, 768), F32),
             pltpu.VMEM((15, 96, 256), BF16),
@@ -435,39 +498,61 @@
             pltpu.VMEM((720, 256), F32),
             pltpu.VMEM((60, 40, 256), F32),
             pltpu.VMEM((56, 40, 256), F32),
-            pltpu.VMEM((54, 48, 256), BF16),
+            pltpu.VMEM((54, 40, 256), F32),
             pltpu.VMEM((2304, 256), BF16),
             pltpu.VMEM((2304, 256), BF16),
-            pltpu.SemaphoreType.DMA((5,)),
+            pltpu.VMEM((2304, 256), BF16),
+            pltpu.VMEM((2304, 256), BF16),
+            pltpu.VMEM((50, 64, 256), BF16),
+            pltpu.VMEM((72, 58 * 64), F32),
+            pltpu.VMEM(seen.shape, BF16),
+            pltpu.VMEM(mats[2].shape, BF16),
+            pltpu.VMEM(mats[3].shape, BF16),
+            pltpu.SemaphoreType.DMA((7,)),
         ],
-        compiler_params=pltpu.CompilerParams(vmem_limit_bytes=VMEM),
+        compiler_params=pltpu.CompilerParams(vmem_limit_bytes=60 * MIB),
         cost_estimate=pl.CostEstimate(flops=1 << 33, bytes_accessed=1 << 23, transcendentals=1 << 21),
-    )(turned, pick, seen, *mats)
+    )(images, pick, seen, *mats, t_grad)
 
 
 def outer_kernel(
-    far_west, west, east, far_east, nat, pick, seen, m_one_in, m_two_in, r_first, r_last, t_force, left, right,
-    act_in, flat_in,
-    back_three, keep_two, keep_one, basis, gram,
-    window, lhs, lhs_back, pre, wet, back_pre, act_one, act_two, tl_three, buf_a, buf_b, flat, turn, m_one, m_two, sems,
+    far_west, west, east, far_east, images, pick, seen_in, m_one_in, m_two_in, r_first_in, r_last_in, t_force,
+    left_in, right_in, act_in, force_in,
+    back_out, two_out, one_out, basis, gram,
+    window, lhs, lhs_back, pre, wet, back_pre, act_one, act_two, tl_three, buf_a, buf_b, flat, turn, m_one, m_two,
+    nat, left, right, image, keep_one, keep_two, back_three, seen, r_first, r_last, sems,
 ):
-    loads = [copy(m_one_in, m_one, sems.at[2]), copy(m_two_in, m_two, sems.at[3])]
-    moves = [
-        copy(flat_in, flat.at[:, 512 : 512 + 54 * 64], sems.at[0]),
-        copy(act_in, act_two.at[8:12], sems.at[1]),
+    tables = [
+        copy(r_first_in, r_first, sems.at[10]),
+        copy(seen_in, seen, sems.at[11]),
+        copy(r_last_in, r_last, sems.at[12]),
+    ]
+    load_one = copy(m_one_in, m_one, sems.at[2])
+    load_act = copy(act_in, act_two.at[8:12], sems.at[3])
+    load_two = copy(m_two_in, m_two, sems.at[4])
+    late = [
+        copy(images.at[6:9, 0 : nat.shape[1]], nat, sems.at[5]),
+        copy(left_in, left, sems.at[6]),
+        copy(right_in, right, sems.at[7]),
+        copy(force_in, image, sems.at[8]),
     ]
     sel = pick[...]
+    tl_three[:, 48:64] = jnp.zeros((20, 16, 256), BF16)
+    tl_three[8:12] = jnp.zeros((4, 64, 256), BF16)
+    turn[...] = jnp.zeros(turn.shape, F32)
     for c in range(6):
         strips = [far_west[c], west[c], east[c], far_east[c]]
         window[c] = mm(jnp.concatenate(strips, axis=0).astype(BF16), sel)
-    tl_three[:, 48:64] = jnp.zeros((16, 16, 256), BF16)
     for k in range(6):
         slab(window, (0, 8, 16, 32, 40, 48)[k], k, lhs, lhs_back)
+    for move in tables:
+        move.wait()
     first_products(lhs, lhs_back, seen, r_first, r_last, pre, wet, back_pre, 0, 6)
     for k in range(6):
         for jj in range(4):
             first_finish(k, jj, pre, wet, act_one.at[k * 4 + jj], keep_one.at[k * 4 + jj])
-    loads[0].wait()
+    sends = [copy(keep_one.at[6:20], one_out, sems.at[9])]
+    load_one.wait()
 
     def dot_two(q, buf):
         buf[...] = three_taps(act_one, (2, 14)[q], 8, m_one)
@@ -479,10 +564,6 @@
                 buf[jj * 80 : jj * 80 + 80], wet[at % 4, at // 4], act_two.at[(0, 12)[q] + jj], keep_two.at[q * 8 + jj]
             )
 
-    pipeline((8, 8), dot_two, finish_two, (buf_a, buf_b))
-    for move in moves + loads[1:]:
-        move.wait()
-
     def dot_three(q, buf):
         buf[...] = three_taps(act_two, (0, 10)[q], 8, m_two)
 
@@ -491,16 +572,29 @@
             at = (4, 14)[q] + jj
             third_finish(
                 buf[jj * 80 : jj * 80 + 80], wet[at % 4, at // 4], back_pre[at % 4, at // 4],
-                tl_three.at[q * 8 + jj], back_three.at[q * 8 + jj],
+                tl_three.at[q * 12 + jj], back_three.at[q * 8 + jj],
             )
 
-    pipeline((8, 8), dot_three, finish_three, (buf_a, buf_b))
-    thin_taps(t_force[...], tl_three.at[0:8], 8, flat, 0)
-    thin_taps(t_force[...], tl_three.at[8:16], 8, flat, 62 * 64)
-    turn[...] = jnp.zeros(turn.shape, F32)
-    image = thin_sum(flat, 68)
+    dot_two(0, buf_a)
+    dot_two(1, buf_b)
+    finish_two(0, buf_a)
+    load_act.wait()
+    load_two.wait()
+    dot_three(0, buf_a)
+    finish_two(1, buf_b)
+    sends.append(copy(keep_two, two_out, sems.at[13]))
+    dot_three(1, buf_b)
+    finish_three(0, buf_a)
+    thin_taps(t_force[...], tl_three.at[0:10], 10, flat.at[0], 0)
+    finish_three(1, buf_b)
+    sends.append(copy(back_three, back_out, sems.at[14]))
+    thin_taps(t_force[...], tl_three.at[10:20], 10, flat.at[1], 0)
+    for move in late:
+        move.wait()
+    image[:, 0:512] += thin_sum(flat.at[0], 8)
+    image[:, 60 * 64 :] += thin_sum(flat.at[1], 8)
     tall = nat.shape[1]
-    force = unfold(image, 0, 40, tall, left[...], right, turn)
+    force = unfold(image[...], 1, 64, left[...], right[...], turn)
     gap = jnp.zeros((128 - 2 * HALO, 128), F32)
 
     def wide(c):
@@ -528,31 +622,33 @@
     inner = [v[HALO : tall - HALO, 0:128] for v in (v0, v1, v2, v3)]
     for k in range(4):
         basis[k] = inner[k]
-    lane = lax.broadcasted_iota(jnp.int32, (8, 128), 1)
-    sums = jnp.zeros((8, 128), F32)
-    at = 0
+    sums = []
     for i in range(4):
         for j in range(i, 4):
-            prod = jnp.sum(inner[i] * inner[j], axis=0, keepdims=True)
-            value = jnp.sum(prod, axis=1, keepdims=True)
-            sums = jnp.where(lane == at, value, sums)
-            at += 1
+            sums.append(jnp.sum(inner[i] * inner[j], axis=0, keepdims=True))
+    sums.append(jnp.zeros((16 - len(sums), 128), F32))
+    sums = jnp.sum(jnp.concatenate(sums, axis=0), axis=1, keepdims=True)
+    row = lax.broadcasted_iota(jnp.int32, (16, 128), 0)
+    lane = lax.broadcasted_iota(jnp.int32, (16, 128), 1)
+    sums = jnp.sum(jnp.where(row == lane, sums, 0.0), axis=0, keepdims=True)
     gram[...] = jnp.broadcast_to(sums, gram.shape)
-
-
-def outer_pass(strips, nat, pick, seen, mats, left, right, act_in, flat_in, devices):
-    tall = nat.shape[1]
+    for send in sends:
+        send.wait()
+
+
+def outer_pass(strips, images, tall, pick, seen, mats, left, right, act_in, force_in, devices):
     return pl.pallas_call(
         outer_kernel,
         name="outer_pass",
         out_shape=(
-            jax.ShapeDtypeStruct((16, 48, 256), BF16),
             jax.ShapeDtypeStruct((16, 40, 256), F32),
-            jax.ShapeDtypeStruct((24, 40, 256), F32),
+            jax.ShapeDtypeStruct((16, 40, 256), F32),
+            jax.ShapeDtypeStruct((14, 40, 256), F32),
             jax.ShapeDtypeStruct((4, tall - 2 * HALO, 128), F32),
-            jax.ShapeDtypeStruct((devices, 8, 128), F32),
+            jax.ShapeDtypeStruct((devices, 1, 128), F32),
         ),
-        in_specs=[HERE] * 7 + [ANY, ANY] + [HERE] * 5 + [ANY, ANY],
+        in_specs=[HERE, HERE, HERE, HERE, ANY, HERE, ANY, ANY, ANY, ANY, ANY, HERE, ANY, ANY, ANY, ANY],
+        out_specs=(ANY, ANY, ANY, HERE, HERE),
         scratch_shapes=[
             pltpu.VMEM((6, 64, 768), F32),
             pltpu.VMEM((6, 96, 256), BF16),
@@ -562,122 +658,116 @@
             pltpu.VMEM((4, 6, 48, 256), F32),
             pltpu.VMEM((24, 80, 768), BF16),
             pltpu.VMEM((20, 80, 768), BF16),
-            pltpu.VMEM((16, 64, 256), BF16),
+            pltpu.VMEM((20, 64, 256), BF16),
             pltpu.VMEM((640, 256), F32),
             pltpu.VMEM((640, 256), F32),
-            pltpu.VMEM((72, 70 * 64), F32),
-            pltpu.VMEM((320, 128), F32),
+            pltpu.VMEM((2, 72, 10 * 64), F32),
+            pltpu.VMEM((512, 128), F32),
             pltpu.VMEM((2304, 256), BF16),
             pltpu.VMEM((2304, 256), BF16),
-            pltpu.SemaphoreType.DMA((4,)),
+            pltpu.VMEM((3, tall, 128), F32),
+            pltpu.VMEM(left.shape, F32),
+            pltpu.VMEM(right.shape, F32),
+            pltpu.VMEM((8, 68 * 64), F32),
+            pltpu.VMEM((24, 40, 256), F32),
+            pltpu.VMEM((16, 40, 256), F32),
+            pltpu.VMEM((16, 40, 256), F32),
+            pltpu.VMEM(seen.shape, BF16),
+            pltpu.VMEM(mats[2].shape, BF16),
+            pltpu.VMEM(mats[3].shape, BF16),
+            pltpu.SemaphoreType.DMA((15,)),
         ],
-        compiler_params=pltpu.CompilerParams(vmem_limit_bytes=VMEM),
+        compiler_params=pltpu.CompilerParams(vmem_limit_bytes=60 * MIB),
         cost_estimate=pl.CostEstimate(flops=1 << 32, bytes_accessed=1 << 23, transcendentals=1 << 20),
-    )(*strips, nat, pick, seen, *mats, left, right, act_in, flat_in)
+    )(*strips, images, pick, seen, *mats, left, right, act_in, force_in)
 
 
 def adjoint_kernel(
-    back_in, back_rim, two_in, two_rim, one_in, one_rim, m_one_in, m_two_in, t_grad, left, right,
+    back_in, back_rim, two_in, two_rim, one_in, one_rim, m_one_in, m_two_in, t_grad, left, right, grad_in,
     grad,
-    back_three, keep_two, keep_one, three, two, one, buf_a, buf_b, flat, turn, m_one, m_two, m_one_t, m_two_t, sems,
+    back_three, keep_two, keep_one, three, two, one, buf_a, buf_b, flat, turn, m_one_t, m_two_t, image, sems,
 ):
-    load_two = copy(m_two_in, m_two, sems.at[3, 0])
-    def load(inside, rim, target, first, count, pieces, sem):
-        moves = [copy(inside, target.at[first : first + count], sem.at[0])]
-        for k, (start, stop, to) in enumerate(pieces):
-            moves.append(copy(rim.at[start:stop], target.at[to : to + stop - start], sem.at[k + 1]))
-        return moves
-
-    moves_three = load(back_in, back_rim, back_three, 8, 54, ((0, 8, 0), (8, 16, 62)), sems.at[0])
-    moves_two = load(two_in, two_rim, keep_two, 8, 56, ((0, 8, 0), (8, 16, 64)), sems.at[1])
-    moves_one = load(one_in, one_rim, keep_one, 8, 60, ((0, 8, 0), (16, 24, 68)), sems.at[2])
-    load_one = copy(m_one_in, m_one, sems.at[3, 1])
-
-    def turn_over(source, target):
-        for tap in range(9):
-            target[(8 - tap) * 256 : (9 - tap) * 256, :] = source[tap * 256 : tap * 256 + 256, :].T
-
-    load_two.wait()
-    turn_over(m_two, m_two_t)
+    moves_three = [
+        copy(back_rim.at[0:8], back_three.at[0, 0:8], sems.at[0]),
+        copy(back_in.at[0:4], back_three.at[0, 8:12], sems.at[1]),
+        copy(back_in.at[4:8], back_three.at[1, 0:4], sems.at[2]),
+        copy(back_rim.at[8:16], back_three.at[1, 4:12], sems.at[3]),
+        copy(m_two_in, m_two_t, sems.at[4]),
+    ]
+    moves_two = [
+        copy(two_rim.at[2:8], keep_two.at[0, 0:6], sems.at[5]),
+        copy(two_in.at[0:4], keep_two.at[0, 6:10], sems.at[6]),
+        copy(two_in.at[4:8], keep_two.at[1, 0:4], sems.at[7]),
+        copy(two_rim.at[8:14], keep_two.at[1, 4:10], sems.at[8]),
+        copy(m_one_in, m_one_t, sems.at[9]),
+    ]
+    moves_one = [
+        copy(one_rim.at[0:6], keep_one.at[0, 0:6], sems.at[10]),
+        copy(one_in, keep_one.at[0, 6:8], sems.at[11]),
+        copy(one_rim.at[6:14], keep_one.at[1], sems.at[12]),
+        copy(grad_in, image, sems.at[13]),
+    ]
+    one[:, 48:64] = jnp.zeros((20, 16, 256), BF16)
+    one[8:12] = jnp.zeros((4, 64, 256), BF16)
     for move in moves_three:
         move.wait()
-
-    def spread(s, _):
-        spread_rows(three.at[s], back_three[s].astype(F32)[0:40], back_three[s + 32].astype(F32)[0:40])
-        return 0
-
-    lax.fori_loop(0, 38, spread, 0, unroll=2)
-    load_one.wait()
-    turn_over(m_one, m_one_t)
+    for s in range(12):
+        spread_rows(three.at[s], back_three[0, s], back_three[1, s])
+    buf_a[...] = three_taps(three, 0, 10, m_two_t)
     for move in moves_two:
         move.wait()
-
-    def dot_two(q, buf):
-        buf[...] = three_taps(three, q * 9, 9, m_two_t)
-
-    def finish_two(q, buf):
-        for jj in range(9):
-            s = q * 9 + jj
-            x0 = buf[jj * 80 : jj * 80 + 40] * keep_two[s + 2]
-            x1 = buf[jj * 80 + 40 : jj * 80 + 80] * keep_two[s + 34]
-            spread_rows(two.at[s], x0, x1)
-
-    pipeline((9, 9, 9, 9), dot_two, finish_two, (buf_a, buf_b))
-    one[:, 48:64] = jnp.zeros((66, 16, 256), BF16)
+    for s in range(10):
+        x0 = buf_a[s * 80 : s * 80 + 40] * keep_two[0, s]
+        x1 = buf_a[s * 80 + 40 : s * 80 + 80] * keep_two[1, s]
+        spread_rows(two.at[s], x0, x1)
+    buf_b[...] = three_taps(two, 0, 8, m_one_t)
     rest = jnp.zeros((8, 256), F32)
     for move in moves_one:
         move.wait()
-    sizes = (9, 9, 8, 8)
-
-    def dot_one(q, buf):
-        buf[0 : sizes[q] * 80] = three_taps(two, sum(sizes[:q]), sizes[q], m_one_t)
-
-    def finish_one(q, buf):
-        for jj in range(sizes[q]):
-            s = sum(sizes[:q]) + jj
-            x0 = buf[jj * 80 : jj * 80 + 40] * keep_one[s + 6]
-            x1 = buf[jj * 80 + 40 : jj * 80 + 80] * keep_one[s + 38]
-            one[s, 0:48] = jnp.concatenate([x0, rest], axis=0).astype(BF16)
-            one[s + 32, 0:48] = jnp.concatenate([x1, rest], axis=0).astype(BF16)
-
-    pipeline(sizes, dot_one, finish_one, (buf_a, buf_b))
-    thin_taps(t_grad[...], one, 66, flat, 0)
-    image = thin_sum(flat, 64)
+    for s in range(8):
+        x0 = buf_b[s * 80 : s * 80 + 40] * keep_one[0, s]
+        x1 = buf_b[s * 80 + 40 : s * 80 + 80] * keep_one[1, s]
+        one[s, 0:48] = jnp.concatenate([x0, rest], axis=0).astype(BF16)
+        one[s + 12, 0:48] = jnp.concatenate([x1, rest], axis=0).astype(BF16)
+    thin_taps(t_grad[...], one.at[0:10], 10, flat.at[0], 0)
+    thin_taps(t_grad[...], one.at[10:20], 10, flat.at[1], 0)
+    image[:, 0:512] += thin_sum(flat.at[0], 8)
+    image[:, 56 * 64 :] += thin_sum(flat.at[1], 8)
     rows = grad.shape[1]
-    for ch in range(2):
-        grad[ch] = unfold(image, ch * 4, 32, rows, left[...], right, turn)
-
-
-def adjoint_pass(fields, mats, left, right):
+    both = unfold(image[...], 2, 32, left[...], right[...], turn)
+    grad[0] = both[:rows]
+    grad[1] = both[rows:]
+
+
+def adjoint_pass(fields, mats, left, right, grad_in):
     return pl.pallas_call(
         adjoint_kernel,
         name="adjoint_pass",
         out_shape=jax.ShapeDtypeStruct((2, left.shape[0] // 2, 128), F32),
-        in_specs=[ANY] * 8 + [HERE] * 3,
+        in_specs=[ANY] * 8 + [HERE] * 3 + [ANY],
         scratch_shapes=[
-            pltpu.VMEM((70, 48, 256), BF16),
-            pltpu.VMEM((72, 40, 256), F32),
-            pltpu.VMEM((76, 40, 256), F32),
-            pltpu.VMEM((38, 80, 768), BF16),
-            pltpu.VMEM((36, 80, 768), BF16),
-            pltpu.VMEM((66, 64, 256), BF16),
-            pltpu.VMEM((720, 256), F32),
-            pltpu.VMEM((720, 256), F32),
-            pltpu.VMEM((72, 66 * 64), F32),
+            pltpu.VMEM((2, 12, 40, 256), F32),
+            pltpu.VMEM((2, 10, 40, 256), F32),
+            pltpu.VMEM((2, 8, 40, 256), F32),
+            pltpu.VMEM((12, 80, 768), BF16),
+            pltpu.VMEM((10, 80, 768), BF16),
+            pltpu.VMEM((20, 64, 256), BF16),
+            pltpu.VMEM((800, 256), F32),
+            pltpu.VMEM((640, 256), F32),
+            pltpu.VMEM((2, 72, 10 * 64), F32),
             pltpu.VMEM((256, 128), F32),
             pltpu.VMEM((2304, 256), BF16),
             pltpu.VMEM((2304, 256), BF16),
-            pltpu.VMEM((2304, 256), BF16),
-            pltpu.VMEM((2304, 256), BF16),
-            pltpu.SemaphoreType.DMA((4, 3)),
+            pltpu.VMEM((8, 64 * 64), F32),
+            pltpu.SemaphoreType.DMA((14,)),
         ],
-        compiler_params=pltpu.CompilerParams(vmem_limit_bytes=VMEM),
+        compiler_params=pltpu.CompilerParams(vmem_limit_bytes=60 * MIB),
         cost_estimate=pl.CostEstimate(flops=1 << 33, bytes_accessed=1 << 23, transcendentals=0),
-    )(*fields, *mats, left, right)
+    )(*fields, *mats, left, right, grad_in)
 
 
 def combine_kernel(basis, gram, surface, residual):
-    sums = jnp.sum(gram[...], axis=0)[0:1, :]
+    sums = jnp.sum(gram[...], axis=0)
     g = {}
     at = 0
     for i in range(4):
@@ -733,7 +823,10 @@
 
 def combine(basis, gram):
     shape = jax.ShapeDtypeStruct(basis.shape[1:], F32)
-    return pl.pallas_call(combine_kernel, name="combine", out_shape=(shape, shape))(basis, gram)
+    return pl.pallas_call(
+        combine_kernel, name="combine", out_shape=(shape, shape),
+        compiler_params=pltpu.CompilerParams(vmem_limit_bytes=4 * MIB),
+    )(basis, gram)
 
 
 def shards(
@@ -759,20 +852,20 @@
     m_one, m_two, r_first, r_last, t_force, t_grad = fold_weights(
         w_middle_one, w_middle_two, w_first, w_last, (e_first, e_last, e_force, e_grad)
     )
-    turned, nat, west, east = columns_out(own, above, below)
+    images, west, east = columns_out(own, above, below)
     far_west = lax.ppermute(east, "gx", [(i, (i + 1) % gx) for i in range(gx)])
     far_east = lax.ppermute(west, "gx", [((i + 1) % gx, i) for i in range(gx)])
     pick = decimate()
     mats = (m_one, m_two, r_first, r_last, t_force)
-    back_in, two_in, one_in, act_in, flat_in = inner_pass(turned, pick, seen, mats)
-    left, right = unfold_tables(tall, 36, 12, 40, 256, -4)
+    back_in, two_in, one_in, act_in, m_one_t, m_two_t, force_in, grad_in = inner_pass(images, pick, seen, mats, t_grad)
+    left, right = unfold_tables(tall, 36, 12, 64, 256, -4)
     back_rim, two_rim, one_rim, basis, gram = outer_pass(
-        (far_west, west, east, far_east), nat, pick, seen, mats, left, right, act_in, flat_in, gx * gy
+        (far_west, west, east, far_east), images, tall, pick, seen, mats, left, right, act_in, force_in, gx * gy
     )
     gram = lax.all_to_all(gram, ("gx", "gy"), 0, 0)
     left, right = unfold_tables(rows, 32, 0, 32, 128, 0)
     fields = (back_in, back_rim, two_in, two_rim, one_in, one_rim)
-    grad = adjoint_pass(fields, (m_one, m_two, t_grad), left, right)
+    grad = adjoint_pass(fields, (m_one_t, m_two_t, t_grad), left, right, grad_in)
     surface, residual = combine(basis, gram)
     return (grad, surface, residual)
 

time: 71.9 us -> 65 us (0.904)
  Pallas kernels: 53.7 us -> 47.4 us
    pallas_call x1, Pallas kernels: 14.8 us -> 8.24 us  [adjoint_pass(): pl.pallas_call(adjoint_kernel, name='adjoint_pass', out_shape=jax.ShapeDt...]
    pallas_call x1, Pallas kernels: 20.8 us -> 23.6 us  [inner_pass(): pl.pallas_call(inner_kernel, name='inner_pass', out_shape=(jax.ShapeDtype...]
    pallas_call x1, Pallas kernels: 1.93 us -> 0.18 us  [columns_out(): pl.pallas_call(columns_kernel, name='columns_out', out_shape=(jax.ShapeDt...]
    pallas_call x1, Pallas kernels: 1.81 us -> 0.85 us  [combine(): pl.pallas_call(combine_kernel, name='combine', out_shape=(shape, shape),...]
    unnamed x10 -> x14, local copies, waits for them, and re-layouts: 1.91 us -> 1.48 us
where the time goes in v3:
time: 65 us; the launch traced here: 64.6 us
  Pallas kernels  47.4 us (73%)
  starting transfers between devices  14.8 us (23%)
  local copies, waits for them, and re-layouts  1.48 us (2%)
  between operations  0.77 us (1%)
    pallas_call x1, Pallas kernels, inner_pass(): pl.pallas_call(inner_kernel, name='inner_pass', out_shape=(jax.ShapeDtype...  23.6 us
    pallas_call x1, Pallas kernels, outer_pass(): pl.pallas_call(outer_kernel, name='outer_pass', out_shape=(jax.ShapeDtype...  9.04 us
    pallas_call x1, Pallas kernels, adjoint_pass(): pl.pallas_call(adjoint_kernel, name='adjoint_pass', out_shape=jax.ShapeDt...  8.24 us
    all_to_all x1, starting transfers between devices, shards(): gram = lax.all_to_all(gram, ('gx', 'gy'), 0, 0)  5.85 us
    pallas_call x1, Pallas kernels, fold_weights(): pl.pallas_call(weights_kernel, name='fold_weights', out_shape=(big, big,...  3.89 us
    ppermute x1, starting transfers between devices, shards(): far_east = lax.ppermute(west, 'gx', [((i + 1) % gx, i) for i in range(gx)])  3.04 us
    ppermute x1, starting transfers between devices, shards(): above = lax.ppermute(bottom, 'gy', [(i, i + 1) for i in range(gy - 1)])  2.48 us
    ppermute x1, starting transfers between devices, shards(): far_west = lax.ppermute(east, 'gx', [(i, (i + 1) % gx) for i in range(gx)])  2.09 us
  transfers between devices with their start and end apart: 5, of which 1 were waited for; matrix products, arithmetic and copies ran while one was open for 0% of the time, Pallas kernels for 55%

profile of v3, /device:TPU:0, one launch (start us, length us, event | category | flops | bytes accessed | tf_op | source)
XLA Modules:
  0.0 64.6 jit_solution(7581979464201267934)
XLA Ops:
  0.6 1.6 %rows_out.1 = (f32[8,64,128]{2,1,0:T(8,128)}, f32[8,16,128]{2,1,0:T(8,128)}, f32[8,16,128]{2,1,0:T(8,128)}) custom-call(bf16[2,64,128]{2,1,0:T(8,128)(2,1)} %base.1, bf16[2,64,128]{2,1,0:T(8,128)(2,1)} %incr.1, bf16[64,128]{1,0:T(8,128)(2,1)} %cot.1, s32[64,128]{1,0:T(8,128)} %land.1, f32[64,128]{1,0:T(8,128)} %storage.1, f32[64,128]{1,0:T(8,128)} %source.1), custom_call_target="tpu_custom_call" | custom-call | tf_op jit(solution)/shard_map/rows_out/pallas_call | solution.py:184
  2.2 0.0 copy-start
  2.2 2.5 %collective-permute-start = (f32[8,16,128]{2,1,0:T(8,128)}, f32[8,16,128]{2,1,0:T(8,128)S(1)}, u32[]{:S(2)}, u32[]{:S(2)}) collective-permute-start(f32[8,16,128]{2,1,0:T(8,128)} %get-tuple-element.31), channel_id=1, source_target_pairs={{0,1},{1,2},{2,3},{4,5},{5,6},{6,7},{8,9},{9,10},{10,11},{12,13},{... | collective-permute-start | bytes 196616 | tf_op jit(solution)/shard_map/ppermute | solution.py:848
  4.7 1.3 %collective-permute-start.1 = (f32[8,16,128]{2,1,0:T(8,128)}, f32[8,16,128]{2,1,0:T(8,128)S(1)}, u32[]{:S(2)}, u32[]{:S(2)}) collective-permute-start(f32[8,16,128]{2,1,0:T(8,128)} %get-tuple-element.32), channel_id=1, source_target_pairs={{1,0},{2,1},{3,2},{5,4},{6,5},{7,6},{9,8},{10,9},{11,10},{13,12},{... | collective-permute-start | bytes 196616 | tf_op jit(solution)/shard_map/ppermute | solution.py:849
  6.0 3.9 %fold_weights.1 = (bf16[2304,256]{1,0:T(8,128)(2,1)}, bf16[2304,256]{1,0:T(8,128)(2,1)}, bf16[256,1024]{1,0:T(8,128)(2,1)}, bf16[128,1024]{1,0:T(8,128)(2,1)}, b...) custom-call(bf16[25,4096]{1,0:T(8,128)(2,1)} %w_one.1, bf16[25,4096]{1,0:T(8,128)(2,1)} %w_two.1, ...), custom_call_target="tpu_custom_call" | custom-call | flops 16777216 | bytes 8388608 | tf_op jit(solution)/shard_map/fold_weights/pallas_call | solution.py:148
  9.9 0.0 collective-permute-done.above
  9.9 0.3 collective-permute-done.1.below
  10.2 0.0 copy-done
  10.2 0.2 columns_out.1
  10.4 0.0 copy-start.2
  10.4 0.8 %copy-done.2 = f32[9,128,128]{2,1,0:T(8,128)} copy-done((f32[9,128,128]{2,1,0:T(8,128)}, f32[9,128,128]{2,1,0:T(8,128)S(1)}, u32[]{:S(2)}) %copy-start.2) | copy-done | bytes 589848
  11.2 0.0 copy-start.3
  11.2 0.0 copy-start.4
  11.2 2.1 %collective-permute-start.2 = (f32[8,16,128]{2,1,0:T(8,128)S(1)}, f32[8,16,128]{2,1,0:T(8,128)S(1)}, u32[]{:S(2)}, u32[]{:S(2)}) collective-permute-start(f32[8,16,128]{2,1,0:T(8,128)S(1)} %get-tuple-element.41.east), channel_id=1, source_target_pairs={{0,4},{4,8},{8,12},{12,16},{16,20},{20,24},{24,28},{28,0},{1,5},{5... | collective-permute-start | bytes 196616 | tf_op jit(solution)/shard_map/ppermute | solution.py:856
  13.3 3.0 %collective-permute-start.3 = (f32[8,16,128]{2,1,0:T(8,128)S(1)}, f32[8,16,128]{2,1,0:T(8,128)S(1)}, u32[]{:S(2)}, u32[]{:S(2)}) collective-permute-start(f32[8,16,128]{2,1,0:T(8,128)S(1)} %get-tuple-element.42.west), channel_id=1, source_target_pairs={{4,0},{8,4},{12,8},{16,12},{20,16},{24,20},{28,24},{0,28},{5,1},{9... | collective-permute-start | bytes 196616 | tf_op jit(solution)/shard_map/ppermute | solution.py:857
  16.4 23.6 %inner_pass.1 = (f32[8,40,256]{2,1,0:T(8,128)}, f32[8,40,256]{2,1,0:T(8,128)}, f32[2,40,256]{2,1,0:T(8,128)}, bf16[4,80,768]{2,1,0:T(8,128)(2,1)}, bf16[2304,256...) custom-call(f32[9,128,128]{2,1,0:T(8,128)} %copy-done.2, ...), custom_call_target="tpu_custom_call" | custom-call | flops 8589934592 | bytes 8388608 | tf_op jit(solution)/shard_map/inner_pass/pallas_call | solution.py:472
  39.9 0.0 copy-done.3
  39.9 0.0 copy-done.4
  40.0 0.0 collective-permute-done.2.far_west
  40.0 0.0 copy-start.5
  40.0 0.0 collective-permute-done.3.far_east
  40.0 0.0 copy-start.6
  40.0 0.6 copy-done.5
  40.6 0.0 copy-done.6
  40.6 9.0 %outer_pass.1 = (f32[16,40,256]{2,1,0:T(8,128)}, f32[16,40,256]{2,1,0:T(8,128)}, f32[14,40,256]{2,1,0:T(8,128)}, f32[4,64,128]{2,1,0:T(8,128)}, f32[32,1,128]{2,1,0:T(1,128)}) custom-call(f32[8,16,128]{2,1,0:T(8,128)} %copy-done.5, f32[8,16,128]{2,1,0:T(8,128)} %copy-done.3, f32[8,16,128]{2,1,0:T(8,128)} %copy-done.4, f32[8,16,128]{2,1,0:T(8,128)} %copy-done.6, ...), custom_call_target="tpu_custom_call" | custom-call | flops 4294967296 | bytes 8388608 | tf_op jit(solution)/shard_map/outer_pass/pallas_call | solution.py:640
  49.7 5.9 %all-to-all-start = ((f32[32,1,128]{2,1,0:T(1,128)}), f32[32,1,128]{2,1,0:T(1,128)S(1)}, u32[]{:S(2)}, u32[]{:S(2)}) async-start(f32[32,1,128]{2,1,0:T(1,128)} %get-tuple-element.54), calls=%async_computation | async-start | bytes 32768 | tf_op jit(solution)/shard_map/all_to_all | solution.py:865
  55.5 0.0 copy-start.1
  55.5 8.2 %adjoint_pass.1 = f32[2,64,128]{2,1,0:T(8,128)} custom-call(f32[8,40,256]{2,1,0:T(8,128)} %get-tuple-element.40.back_in, f32[16,40,256]{2,1,0:T(8,128)} %get-tuple-element.45.back_rim, f32[8,40,256]{2,1,0:T(8,128)} %get-tuple-element.46.two_in, f32[16,40,256]{2,1,0:T(8,128)} %get-tuple-element.47.two_rim, f32[2,40,256]{2,1,0:T(8,128)} %get-tuple-element.48.one_in, ...), custom_call_target="tpu_custom_call" | custom-call | flops 8589934592 | bytes 8388608 | tf_op jit(solution)/shard_map/adjoint_pass/pallas_call | solution.py:743
  63.8 0.0 all-to-all-done.gram
  63.8 0.0 copy-done.1
  63.8 0.8 %combine.1 = (f32[64,128]{1,0:T(8,128)}, f32[64,128]{1,0:T(8,128)}) custom-call(f32[4,64,128]{2,1,0:T(8,128)S(1)} %copy-done.1, f32[32,1,128]{2,1,0:T(1,128)S(1)} %all-to-all-done.gram), custom_call_target="tpu_custom_call" | custom-call | tf_op jit(solution)/shard_map/combine/pallas_call | solution.py:826
Async XLA Ops:
  2.2 8.0 %copy-start = (f32[8,64,128]{2,1,0:T(8,128)S(1)}, f32[8,64,128]{2,1,0:T(8,128)}, u32[]{:S(2)}) copy-start(f32[8,64,128]{2,1,0:T(8,128)} %get-tuple-element.30.own) | copy-start | bytes 786436
  2.2 7.7 %collective-permute-start = (f32[8,16,128]{2,1,0:T(8,128)}, f32[8,16,128]{2,1,0:T(8,128)S(1)}, u32[]{:S(2)}, u32[]{:S(2)}) collective-permute-start(f32[8,16,128]{2,1,0:T(8,128)} %get-tuple-element.31), channel_id=1, source_target_pairs={{0,1},{1,2},{2,3},{4,5},{5,6},{6,7},{8,9},{9,10},{10,11},{12,13},{... | collective-permute-start | bytes 196616 | tf_op jit(solution)/shard_map/ppermute | solution.py:848
  4.7 5.5 %collective-permute-start.1 = (f32[8,16,128]{2,1,0:T(8,128)}, f32[8,16,128]{2,1,0:T(8,128)S(1)}, u32[]{:S(2)}, u32[]{:S(2)}) collective-permute-start(f32[8,16,128]{2,1,0:T(8,128)} %get-tuple-element.32), channel_id=1, source_target_pairs={{1,0},{2,1},{3,2},{5,4},{6,5},{7,6},{9,8},{10,9},{11,10},{13,12},{... | collective-permute-start | bytes 196616 | tf_op jit(solution)/shard_map/ppermute | solution.py:849
  10.4 0.9 %copy-start.2 = (f32[9,128,128]{2,1,0:T(8,128)}, f32[9,128,128]{2,1,0:T(8,128)S(1)}, u32[]{:S(2)}) copy-start(f32[9,128,128]{2,1,0:T(8,128)S(1)} %get-tuple-element.33.images) | copy-start | bytes 1769476
  11.2 28.7 %copy-start.3 = (f32[8,16,128]{2,1,0:T(8,128)}, f32[8,16,128]{2,1,0:T(8,128)S(1)}, u32[]{:S(2)}) copy-start(f32[8,16,128]{2,1,0:T(8,128)S(1)} %get-tuple-element.42.west) | copy-start | bytes 196612
  11.2 28.7 %copy-start.4 = (f32[8,16,128]{2,1,0:T(8,128)}, f32[8,16,128]{2,1,0:T(8,128)S(1)}, u32[]{:S(2)}) copy-start(f32[8,16,128]{2,1,0:T(8,128)S(1)} %get-tuple-element.41.east) | copy-start | bytes 196612
  11.2 28.7 %collective-permute-start.2 = (f32[8,16,128]{2,1,0:T(8,128)S(1)}, f32[8,16,128]{2,1,0:T(8,128)S(1)}, u32[]{:S(2)}, u32[]{:S(2)}) collective-permute-start(f32[8,16,128]{2,1,0:T(8,128)S(1)} %get-tuple-element.41.east), channel_id=1, source_target_pairs={{0,4},{4,8},{8,12},{12,16},{16,20},{20,24},{24,28},{28,0},{1,5},{5... | collective-permute-start | bytes 196616 | tf_op jit(solution)/shard_map/ppermute | solution.py:856
  13.3 26.7 %collective-permute-start.3 = (f32[8,16,128]{2,1,0:T(8,128)S(1)}, f32[8,16,128]{2,1,0:T(8,128)S(1)}, u32[]{:S(2)}, u32[]{:S(2)}) collective-permute-start(f32[8,16,128]{2,1,0:T(8,128)S(1)} %get-tuple-element.42.west), channel_id=1, source_target_pairs={{4,0},{8,4},{12,8},{16,12},{20,16},{24,20},{28,24},{0,28},{5,1},{9... | collective-permute-start | bytes 196616 | tf_op jit(solution)/shard_map/ppermute | solution.py:857
  40.0 0.6 copy-start.5
  40.0 0.6 copy-start.6
  49.7 14.1 %all-to-all-start = ((f32[32,1,128]{2,1,0:T(1,128)}), f32[32,1,128]{2,1,0:T(1,128)S(1)}, u32[]{:S(2)}, u32[]{:S(2)}) async-start(f32[32,1,128]{2,1,0:T(1,128)} %get-tuple-element.54), calls=%async_computation | async-start | bytes 32768 | tf_op jit(solution)/shard_map/all_to_all | solution.py:865
  55.5 8.3 %copy-start.1 = (f32[4,64,128]{2,1,0:T(8,128)S(1)}, f32[4,64,128]{2,1,0:T(8,128)}, u32[]{:S(2)}) copy-start(f32[4,64,128]{2,1,0:T(8,128)} %get-tuple-element.53.basis) | copy-start | bytes 393220
